TPU v7x, 128 devices: a whole 4x4x4 slice. The times are simulated.
128 devices in a mesh: req: 8 (over x, core), score: 16 (over z, y).
Axes of the slice: x: 4, y: 4, z: 4, core: 2. Of those that a mesh axis runs over, the one named last changes fastest.
Arguments:
- cand_ids: int32 [32, 2048], P('req', 'score'), may hold values from 0 to 131071, as said below
- table_slab: bfloat16 [131072, 1024], P(('req', 'score')), may hold values from -6 to 6
- user_rows: bfloat16 [32, 1024], P('req', 'score'), may hold values from -6 to 6
- cross_weight: bfloat16 [2, 2048, 2048], replicated, may hold values from -0.125 to 0.125
- cross_bias: float32 [2, 2048], replicated, may hold values from -3 to 3
- hidden_weight: bfloat16 [2048, 1024], replicated, may hold values from -0.125 to 0.125
- hidden_bias: float32 [1024], replicated, may hold values from -3 to 3
- out_weight: bfloat16 [1024], replicated, may hold values from -0.1875 to 0.1875
Outputs:
- scores: float32 [32, 2048], P('req', 'score')
Inputs may be any that keep to these rules, and one draw needn't show every extreme that they name: `cand_ids`: table rows d * 1024 to (d + 1) * 1024 - 1 lie on device d of req+score. Of the candidates of one device, at most 8 lie on the rows of any one device, and some device's rows hold exactly 8 candidates of every device. Ids may repeat.
All inputs are finite; a program needn't handle non-finite values.
Results may differ from a plain program's by a relative error of at most 0.0039.
Values may be sent and summed in bfloat16 or wider, within the bound.
No kernel may reach another device: no remote copies, remote signals or barrier semaphores. Data moves between devices by JAX's collectives and lax.ppermute only.
A program may use at most 128 MiB of HBM per device.

v0:
```python
import jax
import jax.numpy as jnp
from jax import lax
from jax.sharding import PartitionSpec as P


def network(first, cross_weight, cross_bias, hidden_weight, hidden_bias, out_weight):
    first_float = first.astype(jnp.float32)
    state = first_float
    for layer_index in range(cross_weight.shape[0]):
        mixed = jnp.dot(
            state.astype(jnp.bfloat16),
            cross_weight[layer_index],
            preferred_element_type=jnp.float32,
        )
        state = first_float * (mixed + cross_bias[layer_index]) + state
    hidden = jnp.dot(state.astype(jnp.bfloat16), hidden_weight, preferred_element_type=jnp.float32)
    hidden = jax.nn.relu(hidden + hidden_bias).astype(jnp.bfloat16)
    logit = jnp.dot(hidden, out_weight, preferred_element_type=jnp.float32)
    return jax.nn.sigmoid(logit)


def per_device(
    cand_ids,
    table_slab,
    user_rows,
    cross_weight,
    cross_bias,
    hidden_weight,
    hidden_bias,
    out_weight,
):
    req_groups, per_request = cand_ids.shape
    row_count = req_groups * per_request
    devices = lax.axis_size("req") * lax.axis_size("score")
    capacity = max(2, 2 * row_count // devices)
    slab_rows = table_slab.shape[0]
    item_width = table_slab.shape[1]
    flat_ids = cand_ids.reshape(row_count)
    owner_dev = flat_ids // slab_rows
    local_row = flat_ids % slab_rows
    onehot = (owner_dev[:, None] == jnp.arange(devices, dtype=jnp.int32)[None, :]).astype(jnp.int32)
    running = jnp.cumsum(onehot, axis=0)
    slot_rank = jnp.sum(onehot * running, axis=1) - 1
    slot_index = owner_dev * capacity + slot_rank
    send_ids = jnp.full((devices * capacity,), -1, jnp.int32).at[slot_index].set(local_row)
    user_full = lax.all_gather(user_rows, "score", axis=1, tiled=True)
    wanted = lax.all_to_all(
        send_ids.reshape(devices, capacity),
        ("req", "score"),
        split_axis=0,
        concat_axis=0,
        tiled=True,
    )
    valid = wanted >= 0
    fetched = table_slab[jnp.maximum(wanted, 0)]
    answers = jnp.where(valid[..., None], fetched, jnp.zeros_like(fetched))
    returned = lax.all_to_all(answers, ("req", "score"), split_axis=0, concat_axis=0, tiled=True)
    items = returned.reshape(devices * capacity, item_width)[slot_index]
    user_rep = jnp.broadcast_to(
        user_full[:, None, :], (req_groups, per_request, user_full.shape[1])
    )
    user_rep = user_rep.reshape(row_count, user_full.shape[1])
    first = jnp.concatenate([user_rep, items], axis=1)
    scores = network(first, cross_weight, cross_bias, hidden_weight, hidden_bias, out_weight)
    return scores.reshape(req_groups, per_request)


def solution(mesh):
    placed = (
        P("req", "score"),
        P(("req", "score"), None),
        P("req", "score"),
        P(),
        P(),
        P(),
        P(),
        P(),
    )
    return jax.shard_map(
        per_device, mesh=mesh, in_specs=placed, out_specs=P("req", "score"), check_vma=False
    )
```

profile of v0, /device:TPU:4, one launch (start us, length us, event | category | flops | bytes accessed | tf_op | source)
XLA Modules:
  0.0 114.1 jit_solution(746634691917534545)
XLA Ops:
  0.0 0.0 copy-start
  0.0 0.8 add_select_fusion.1
  0.8 0.7 add_select_fusion
  1.5 0.1 copy.18
  1.6 0.2 fusion.24
  2.0 0.2 fusion.23
  2.2 0.7 compare_select_fusion
  2.9 2.4 %scatter_custom_fusion = s32[1024]{0:T(1024)S(1)} fusion(s32[512]{0:T(512)S(1)} %bitcast.80, s32[512]{0:T(512)S(1)} %get-tuple-element.7, s32[]{:T(128)} %constant.41.clone.1), kind=kCustom, calls=%fused_computation.53 | custom fusion | bytes 4100 | tf_op jit(solution)/shard_map/scatter | solution.py:46
  5.4 0.1 all_to_all.9
  5.5 18.0 %all_to_all.14 = s32[128,1,8]{2,1,0:T(1,128)S(1)} all-to-all(s32[128,1,8]{2,1,0:T(1,128)S(1)} %bitcast.75), channel_id=1, replica_groups=mesh['req'=8,'score'=16] {'req','score'}, dimensions={0} | all-to-all | bytes 8192 | tf_op jit(solution)/shard_map/all_to_all | solution.py:48
  23.5 0.1 copy.24
  23.7 0.1 reshape.166
  23.8 0.1 copy.22
  23.9 0.0 copy-done
  23.9 5.4 %gather_fusion = bf16[1024,1024]{1,0:T(8,128)(2,1)} fusion(bf16[1024,1024]{1,0:T(8,128)(2,1)S(1)} %copy-done, s32[1024]{0:T(1024)S(1)} %broadcast_clamp_fusion), kind=kCustom, calls=%fused_computation | custom fusion | bytes 4198400 | tf_op jit(solution)/shard_map/gather | solution.py:56
  29.3 0.0 copy-start.4
  29.3 0.0 copy-start.3
  29.3 0.0 copy-start.2
  29.3 3.2 %bitcast_select_fusion = bf16[128,8,1024]{2,1,0:T(8,128)(2,1)} fusion(bf16[1024,1024]{1,0:T(8,128)(2,1)} %gather_fusion, pred[128,8]{1,0:T(8,128)(4,1)S(1)} %copy.22), kind=kLoop, calls=%fused_computation.16 | loop fusion | flops 1048576 | bytes 4195328 | tf_op jit(solution)/shard_map/jit(_where)/select_n | solution.py:57
  32.5 7.3 %all-to-all-start.1 = ((bf16[128,8,1024]{2,1,0:T(8,128)(2,1)}), bf16[128,8,1024]{2,1,0:T(8,128)(2,1)}, u32[]{:S(2)}, u32[]{:S(2)}) async-start(bf16[128,8,1024]{2,1,0:T(8,128)(2,1)} %bitcast_select_fusion), calls=%async_computation.1 | async-start | bytes 4194304 | tf_op jit(solution)/shard_map/all_to_all | solution.py:58
  39.9 0.0 copy-done.4
  39.9 41.9 %all-gather = bf16[16,64,4]{1,2,0:T(4,128)(2,1)S(1)} all-gather(bf16[1,64,4]{1,2,0:T(4,128)(2,1)S(1)} %bitcast.85), channel_id=1, replica_groups=mesh['req'=8,'score'=16] {'score'}, dimensions={0}, use_global_device_ids=true | all-gather | bytes 8704 | tf_op jit(solution)/shard_map/all_gather | solution.py:47
  81.7 0.1 reshape.191
  81.8 0.0 copy-done.3
  81.9 0.0 copy-done.2
  81.9 0.0 all-to-all-done.1
  81.9 4.6 %gather_fusion.1 = bf16[512,1024]{1,0:T(8,128)(2,1)S(1)} fusion(bf16[1024,1024]{1,0:T(8,128)(2,1)} %bitcast.14, s32[1024]{0:T(1024)S(1)} %pad_clamp_fusion), kind=kCustom, calls=%fused_computation.1 | custom fusion | bytes 2099200 | tf_op jit(solution)/shard_map/gather | solution.py:59
  86.5 0.1 broadcast_in_dim.14
  86.6 0.0 copy-start.1
  86.6 0.0 copy-start.5
  86.6 9.8 %fusion.2 = f32[512,2048]{1,0:T(8,128)} fusion(bf16[2,2048,2048]{2,1,0:T(8,128)(2,1)} %param.11, bf16[512,1024]{1,0:T(8,128)(2,1)S(1)} %gather_fusion.1, bf16[512,1024]{1,0:T(8,128)(2,1)S(1)} %bitcast.72), kind=kOutput, calls=%fused_computation.5 | convolution fusion | flops 4299161600 | bytes 14680064 | tf_op jit(solution)/shard_map/dot_general | solution.py:11
  96.4 0.0 copy-done.1
  96.4 0.0 copy-done.5
  96.4 15.4 %maximum_convert_fusion = bf16[512,1024]{1,0:T(8,128)(2,1)} fusion(bf16[2048,1024]{1,0:T(8,128)(2,1)} %param.13, f32[512,2048]{1,0:T(8,128)} %fusion.2, bf16[2,2048,2048]{2,1,0:T(8,128)(2,1)} %param.11, f32[2048]{0:T(1024)S(1)} %bitcast.84, f32[2048]{0:T(1024)S(1)} %bitcast.83, bf16[512,1024]{1,0:T(8,128)(2,1)S(1)} %gather_fusion.1, ...), kind=kOutput, calls=%fused_computation.17 | convolution fusion | flops 6463946752 | bytes 26243072 | tf_op jit(solution)/shard_map/dot_general | solution.py:17
  111.8 1.6 %fusion.37 = f32[1,512]{1,0:T(1,128)S(1)} fusion(bf16[512,1024]{1,0:T(8,128)(2,1)} %maximum_convert_fusion, bf16[1024,1]{0,1:T(2,128)(2,1)S(1)} %reshape.192), kind=kOutput, calls=%fused_computation.62 | convolution fusion | flops 1048576 | bytes 1052672 | tf_op jit(solution)/shard_map/dot_general | solution.py:19
  113.4 0.6 divide_bitcast_fusion
  (15 shorter events, 0.2 us)
Async XLA Ops:
  0.0 23.9 %copy-start = (bf16[1024,1024]{1,0:T(8,128)(2,1)S(1)}, bf16[1024,1024]{1,0:T(8,128)(2,1)}, u32[]{:S(2)}) copy-start(bf16[1024,1024]{1,0:T(8,128)(2,1)} %param.9) | copy-start | bytes 6291460
  29.3 10.6 %copy-start.4 = (bf16[4,64]{1,0:T(4,128)(2,1)S(1)}, bf16[4,64]{1,0:T(4,128)(2,1)}, u32[]{:S(2)}) copy-start(bf16[4,64]{1,0:T(4,128)(2,1)} %param.10) | copy-start | bytes 1540
  29.3 52.5 %copy-start.3 = (bf16[1024]{0:T(1024)(128)(2,1)S(1)}, bf16[1024]{0:T(1024)(128)(2,1)}, u32[]{:S(2)}) copy-start(bf16[1024]{0:T(1024)(128)(2,1)} %param.15) | copy-start | bytes 6148
  29.3 52.6 %copy-start.2 = (f32[2,2048]{1,0:T(2,128)S(1)}, f32[2,2048]{1,0:T(2,128)}, u32[]{:S(2)}) copy-start(f32[2,2048]{1,0:T(2,128)} %param.12) | copy-start | bytes 49156
  32.5 49.4 %all-to-all-start.1 = ((bf16[128,8,1024]{2,1,0:T(8,128)(2,1)}), bf16[128,8,1024]{2,1,0:T(8,128)(2,1)}, u32[]{:S(2)}, u32[]{:S(2)}) async-start(bf16[128,8,1024]{2,1,0:T(8,128)(2,1)} %bitcast_select_fusion), calls=%async_computation.1 | async-start | bytes 4194304 | tf_op jit(solution)/shard_map/all_to_all | solution.py:58
  86.6 9.8 %copy-start.1 = (bf16[4,128,1024]{2,1,0:T(8,128)(2,1)}, bf16[4,128,1024]{2,1,0:T(8,128)(2,1)S(1)}, u32[]{:S(2)}) copy-start(bf16[4,128,1024]{2,1,0:T(8,128)(2,1)S(1)} %broadcast_in_dim.14) | copy-start | bytes 3145732
  86.6 9.8 %copy-start.5 = (f32[1024]{0:T(1024)S(1)}, f32[1024]{0:T(1024)}, u32[]{:S(2)}) copy-start(f32[1024]{0:T(1024)} %param.14) | copy-start | bytes 12292
where the time goes:
time: 114 us
  blocking collectives  59.9 us (53%)
  matrix products  26.8 us (24%)
  local copies, waits for them, and re-layouts  13.3 us (12%)
  starting transfers between devices  7.35 us (6%)
  other arithmetic  6.57 us (6%)
    all_gather x1, blocking collectives, per_device(): user_full = lax.all_gather(user_rows, 'score', axis=1, tiled=True)  41.9 us
    all_to_all x1, blocking collectives, per_device(): lax.all_to_all(send_ids.reshape(devices, capacity), ('req', 'score'), spl...  18 us
    dot_general x1, matrix products, network(): jnp.dot(state.astype(jnp.bfloat16), hidden_weight, preferred_element_type...  15.4 us
    dot_general x1, matrix products, network(): jnp.dot(state.astype(jnp.bfloat16), cross_weight[layer_index], preferred_...  9.77 us
    all_to_all x1, starting transfers between devices, per_device(): lax.all_to_all(answers, ('req', 'score'), split_axis=0, concat_axis=0, ti...  7.35 us
    gather x1, local copies, waits for them, and re-layouts, per_device(): fetched = table_slab[jnp.maximum(wanted, 0)]  5.39 us
    gather x1, local copies, waits for them, and re-layouts, per_device(): items = returned.reshape(devices * capacity, item_width)[slot_index]  4.59 us
    select_n x1, other arithmetic, per_device(): answers = jnp.where(valid[..., None], fetched, jnp.zeros_like(fetched))  3.21 us
  transfers between devices with their start and end apart: 1, of which 0 were waited for; matrix products, arithmetic and copies ran while one was open for 0% of the time, Pallas kernels for 0%

commit v1 on v0

v1 whole, which is shorter than its diff:
```python
import jax
import jax.numpy as jnp
from jax import lax
from jax.experimental import pallas as pl
from jax.experimental.pallas import tpu as pltpu
from jax.sharding import PartitionSpec as P

BF = jnp.bfloat16
F32 = jnp.float32
AXES = ("req", "score")
CAP = 8
LANES = 128
WORDS = 4


def iota(shape, axis):
    return lax.broadcasted_iota(jnp.int32, shape, axis)


def prepare_kernel(ids_ref, user_ref, msg_ref, key_ref):
    groups, width = ids_ref.shape
    devices = msg_ref.shape[0] // WORDS
    ids = ids_ref[...]
    owner = ids >> 10
    local = ids & 1023
    upto = (iota((width, width), 0) <= iota((width, width), 1)).astype(BF)
    device_row = iota((devices, width), 0)
    base = jnp.zeros((devices, 1), F32)
    high = jnp.zeros((devices, LANES), F32)
    low = jnp.zeros((devices, LANES), F32)
    contract_last = (((1,), (1,)), ((), ()))
    for q in range(groups):
        mine = device_row == owner[q : q + 1, :]
        onehot = mine.astype(BF)
        count = jnp.dot(onehot, upto, preferred_element_type=F32) + base
        rank = jnp.sum(jnp.where(mine, count, 0.0), axis=0, keepdims=True) - 1.0
        rank = rank.astype(jnp.int32)
        base = count[:, width - 1 : width]
        value = local[q : q + 1, :] * groups + (q + 1)
        at_rank = iota((LANES, width), 0) == rank
        value_high = jnp.where(at_rank, value >> 4, 0).astype(F32).astype(BF)
        value_low = jnp.where(at_rank, value & 15, 0).astype(F32).astype(BF)
        high += lax.dot_general(onehot, value_high, contract_last, preferred_element_type=F32)
        low += lax.dot_general(onehot, value_low, contract_last, preferred_element_type=F32)
        key_ref[q : q + 1, :] = owner[q : q + 1, :] * CAP + rank
    user = user_ref[...].astype(F32)
    pairs = [
        jnp.concatenate([user[2 * p : 2 * p + 1, :], user[2 * p + 1 : 2 * p + 2, :]], axis=1)
        for p in range(2)
    ]
    msg_ref[pl.ds(0, devices, stride=WORDS), :] = high * 16.0 + low
    for p in range(2):
        msg_ref[pl.ds(p + 1, devices, stride=WORDS), :] = jnp.broadcast_to(
            pairs[p], (devices, LANES)
        )
    msg_ref[pl.ds(3, devices, stride=WORDS), :] = jnp.zeros((devices, LANES), F32)


def score_kernel(
    msg_ref,
    slab_ref,
    cross_ref,
    cross_bias_ref,
    hidden_ref,
    hidden_bias_ref,
    out_ref,
    score_ref,
    users,
    shift,
    items_hot,
    users_hot,
    first,
    state,
    state_bf,
    logits,
):
    devices = msg_ref.shape[0] // WORDS
    rows = slab_ref.shape[0]
    item_width = slab_ref.shape[1]
    cross = cross_ref.shape[1]
    user_width = cross - item_width
    hid = hidden_ref.shape[1]
    slots = CAP * devices
    per_req = devices // 8
    left = iota((8, LANES), 1) < 64
    for t in range(user_width // LANES):
        for p in range(2):
            even = msg_ref[pl.ds(8 * t + 1 + p, 8, stride=WORDS * per_req), :]
            odd = msg_ref[pl.ds(8 * t + 5 + p, 8, stride=WORDS * per_req), :]
            cols = slice(t * LANES, (t + 1) * LANES)
            users[16 * p : 16 * p + 8, cols] = jnp.where(left, even, pltpu.roll(odd, 64, 1))
            users[16 * p + 8 : 16 * p + 16, cols] = jnp.where(left, pltpu.roll(even, 64, 1), odd)
    users_bf = users[...].astype(BF)
    value = msg_ref[pl.ds(0, devices, stride=WORDS), :].astype(jnp.int32) - 1
    row_of = value >> 2
    req_of = (value & 3) * 8 + iota((devices, LANES), 0) // per_req
    row_lane = iota((devices, rows), 1)
    req_lane = iota((devices, LANES), 1)
    for k in range(CAP):
        part = slice(k * devices, (k + 1) * devices)
        items_hot[part, :] = (row_lane == row_of[:, k : k + 1]).astype(BF)
        users_hot[part, :] = ((req_lane & 31) == req_of[:, k : k + 1]).astype(BF)
    base = jnp.dot(users_bf, cross_ref[0, :user_width, :], preferred_element_type=F32)
    base = base + (cross_bias_ref[0:1, :] + 1.0)
    base_high = base.astype(BF)
    rest = base - base_high.astype(F32)
    base_mid = rest.astype(BF)
    base_low = (rest - base_mid.astype(F32)).astype(BF)
    shift[0:32, :] = base_high
    shift[32:64, :] = base_mid
    shift[64:96, :] = base_low
    shift[96:128, :] = jnp.zeros_like(base_low)
    first[:, :user_width] = jnp.dot(
        users_hot[:, :32], users_bf, preferred_element_type=F32
    ).astype(BF)
    first[:, user_width:] = jnp.dot(
        items_hot[...], slab_ref[...], preferred_element_type=F32
    ).astype(BF)
    tile = 1024

    def layer_one(n, carry):
        cols = pl.ds(pl.multiple_of(n * tile, tile), tile)
        factor = jnp.dot(
            first[:, user_width:], cross_ref[0, user_width:, cols], preferred_element_type=F32
        )
        factor += jnp.dot(users_hot[...], shift[:, cols], preferred_element_type=F32)
        new = first[:, cols].astype(F32) * factor
        state[:, cols] = new
        state_bf[:, cols] = new.astype(BF)
        return carry

    lax.fori_loop(0, cross // tile, layer_one, 0)

    def layer_two(n, carry):
        cols = pl.ds(pl.multiple_of(n * tile, tile), tile)
        mixed = jnp.dot(state_bf[...], cross_ref[1, :, cols], preferred_element_type=F32)
        mixed += cross_bias_ref[1:2, cols]
        state[:, cols] = first[:, cols].astype(F32) * mixed + state[:, cols]
        return carry

    lax.fori_loop(0, cross // tile, layer_two, 0)
    state_bf[...] = state[...].astype(BF)
    hidden = jnp.dot(state_bf[...], hidden_ref[...], preferred_element_type=F32)
    hidden = jnp.maximum(hidden + hidden_bias_ref[...], 0.0).astype(BF)
    logits[...] = jnp.dot(hidden, out_ref[...], preferred_element_type=F32)
    lane = iota((devices, LANES), 1)
    total = jnp.zeros((devices, LANES), F32)
    for k in range(CAP):
        total = jnp.where(lane == k, logits[k * devices : (k + 1) * devices, :], total)
    score_ref[...] = jax.nn.sigmoid(total)


def collect_kernel(scores_ref, key_ref, out_ref):
    groups, width = key_ref.shape
    devices = scores_ref.shape[0]
    scores = scores_ref[...]
    for q in range(groups):
        key = key_ref[q : q + 1, :]
        total = jnp.zeros((devices, width), F32)
        for k in range(CAP):
            here = iota((devices, width), 0) * CAP + k == key
            total += jnp.where(here, scores[:, k : k + 1], 0.0)
        out_ref[q : q + 1, :] = jnp.sum(total, axis=0, keepdims=True)


def per_device(
    cand_ids,
    table_slab,
    user_rows,
    cross_weight,
    cross_bias,
    hidden_weight,
    hidden_bias,
    out_weight,
):
    devices = lax.axis_size("req") * lax.axis_size("score")
    groups, width = cand_ids.shape
    slots = devices * CAP
    cross = cross_weight.shape[1]
    hid = hidden_weight.shape[1]
    vmem = pl.BlockSpec(memory_space=pltpu.VMEM)
    msg, key = pl.pallas_call(
        prepare_kernel,
        out_shape=(
            jax.ShapeDtypeStruct((devices * WORDS, LANES), F32),
            jax.ShapeDtypeStruct((groups, width), jnp.int32),
        ),
        in_specs=[vmem, vmem],
        out_specs=(vmem, vmem),
        name="prepare",
    )(cand_ids, user_rows)
    asked = lax.all_to_all(msg, AXES, split_axis=0, concat_axis=0, tiled=True)
    out_columns = jnp.broadcast_to(out_weight[:, None], (hid, LANES))
    scores = pl.pallas_call(
        score_kernel,
        out_shape=jax.ShapeDtypeStruct((devices, LANES), F32),
        in_specs=[vmem] * 7,
        out_specs=vmem,
        scratch_shapes=[
            pltpu.VMEM((32, cross // 2), F32),
            pltpu.VMEM((LANES, cross), BF),
            pltpu.VMEM((slots, table_slab.shape[0]), BF),
            pltpu.VMEM((slots, LANES), BF),
            pltpu.VMEM((slots, cross), BF),
            pltpu.VMEM((slots, cross), F32),
            pltpu.VMEM((slots, cross), BF),
            pltpu.VMEM((slots, LANES), F32),
        ],
        compiler_params=pltpu.CompilerParams(vmem_limit_bytes=58 * 2**20),
        name="score",
    )(
        asked,
        table_slab,
        cross_weight,
        cross_bias,
        hidden_weight,
        hidden_bias.reshape(1, hid),
        out_columns,
    )
    answered = lax.all_to_all(scores, AXES, split_axis=0, concat_axis=0, tiled=True)
    return pl.pallas_call(
        collect_kernel,
        out_shape=jax.ShapeDtypeStruct((groups, width), F32),
        in_specs=[vmem, vmem],
        out_specs=vmem,
        name="collect",
    )(answered, key)


def solution(mesh):
    placed = (
        P("req", "score"),
        P(("req", "score"), None),
        P("req", "score"),
        P(),
        P(),
        P(),
        P(),
        P(),
    )
    return jax.shard_map(
        per_device, mesh=mesh, in_specs=placed, out_specs=P("req", "score"), check_vma=False
    )
```

time: 114 us -> 75.9 us (0.67)
  the two profiles are of different devices: /device:TPU:4 before, /device:TPU:1 now
where the time goes in v1:
time: 75.9 us; the launch traced here: 75.6 us
  blocking collectives  37.8 us (50%)
  Pallas kernels  36.2 us (48%)
  local copies, waits for them, and re-layouts  1.58 us (2%)
    pallas_call x1, Pallas kernels, per_device(): pl.pallas_call(score_kernel, out_shape=jax.ShapeDtypeStruct((devices, LAN...  32.1 us
    all_to_all x1, blocking collectives, per_device(): asked = lax.all_to_all(msg, AXES, split_axis=0, concat_axis=0, tiled=True)  23.1 us
    all_to_all x1, blocking collectives, per_device(): lax.all_to_all(scores, AXES, split_axis=0, concat_axis=0, tiled=True)  14.8 us
    pallas_call x1, Pallas kernels, per_device(): pl.pallas_call(prepare_kernel, out_shape=(jax.ShapeDtypeStruct((devices *...  2.26 us
    pallas_call x1, Pallas kernels, per_device(): pl.pallas_call(collect_kernel, out_shape=jax.ShapeDtypeStruct((groups, wi...  1.79 us
    broadcast_in_dim x1, local copies, waits for them, and re-layouts, per_device(): out_columns = jnp.broadcast_to(out_weight[:, None], (hid, LANES))  1.58 us

profile of v1, /device:TPU:1, one launch (start us, length us, event | category | flops | bytes accessed | tf_op | source)
XLA Modules:
  0.0 75.6 jit_solution(10497969495383910296)
XLA Ops:
  0.0 2.3 %prepare.1 = (f32[512,128]{1,0:T(8,128)}, s32[4,128]{1,0:T(4,128)}) custom-call(s32[4,128]{1,0:T(4,128)} %ids_ref.1, bf16[4,64]{1,0:T(4,128)(2,1)} %user_ref.1), custom_call_target="tpu_custom_call" | custom-call | tf_op jit(solution)/shard_map/prepare/pallas_call | solution.py:182
  2.3 23.1 %all_to_all.22 = f32[128,4,128]{2,1,0:T(4,128)} all-to-all(f32[128,4,128]{2,1,0:T(4,128)} %bitcast.9), channel_id=1, replica_groups=mesh['req'=8,'score'=16] {'req','score'}, dimensions={0} | all-to-all | bytes 524288 | tf_op jit(solution)/shard_map/all_to_all | solution.py:192
  25.3 1.6 %broadcast_in_dim.2.out_ref = bf16[1024,128]{1,0:T(8,128)(2,1)} broadcast(bf16[1024]{0:T(1024)(128)(2,1)} %param.15), dimensions={0} | broadcast | bytes 264192 | tf_op jit(solution)/shard_map/broadcast_in_dim | solution.py:193
  26.9 32.1 %score.1 = f32[128,128]{1,0:T(8,128)} custom-call(f32[512,128]{1,0:T(8,128)} %bitcast.7, bf16[1024,1024]{1,0:T(8,128)(2,1)} %slab_ref.1, bf16[2,2048,2048]{2,1,0:T(8,128)(2,1)} %cross_ref.1, f32[2,2048]{1,0:T(2,128)} %cross_bias_ref.1, bf16[2048,1024]{1,0:T(8,128)(2,1)} %hidden_ref.1, f32[1,1024]{1,0:T(1,128)} %bitcast.11, ...), custom_call_target="tpu_custom_call" | custom-call | tf_op jit(solution)/shard_map/score/pallas_call | solution.py:194
  59.0 14.8 %all_to_all.23 = f32[128,1,128]{2,1,0:T(1,128)} all-to-all(f32[128,1,128]{2,1,0:T(1,128)} %bitcast.8), channel_id=1, replica_groups=mesh['req'=8,'score'=16] {'req','score'}, dimensions={0} | all-to-all | bytes 131072 | tf_op jit(solution)/shard_map/all_to_all | solution.py:220
  73.8 1.8 %collect.1 = f32[4,128]{1,0:T(4,128)} custom-call(f32[128,128]{1,0:T(8,128)} %bitcast.10, s32[4,128]{1,0:T(4,128)} %get-tuple-element.8.key_ref), custom_call_target="tpu_custom_call" | custom-call | tf_op jit(solution)/shard_map/collect/pallas_call | solution.py:221

commit v2 on v1

--- a/solution.py
+++ b/solution.py
@@ -58,21 +58,26 @@
 
 def score_kernel(
     msg_ref,
-    slab_ref,
-    cross_ref,
+    slab_hbm,
+    cross_hbm,
     cross_bias_ref,
-    hidden_ref,
+    hidden_hbm,
     hidden_bias_ref,
     out_ref,
     score_ref,
+    slab_ref,
+    cross_ref,
+    hidden_ref,
+    copied,
     users,
     shift,
     items_hot,
     users_hot,
     first,
     state,
-    state_bf,
-    logits,
+    state_one,
+    state_two,
+    hidden,
 ):
     devices = msg_ref.shape[0] // WORDS
     rows = slab_ref.shape[0]
@@ -82,6 +87,29 @@
     hid = hidden_ref.shape[1]
     slots = CAP * devices
     per_req = devices // 8
+    half = 512
+    tile = 512
+    parts = [slice(h, h + half) for h in range(0, slots, half)]
+
+    def tiles(width):
+        return [slice(n, n + tile) for n in range(0, width, tile)]
+
+    lower, upper = pl.ds(0, user_width), pl.ds(user_width, item_width)
+    copies = [
+        pltpu.make_async_copy(source, target, copied.at[i])
+        for i, (source, target) in enumerate(
+            [
+                (slab_hbm, slab_ref),
+                (cross_hbm.at[0, lower], cross_ref.at[0, lower]),
+                (cross_hbm.at[0, upper], cross_ref.at[0, upper]),
+                (cross_hbm.at[1], cross_ref.at[1]),
+                (hidden_hbm, hidden_ref),
+            ]
+        )
+    ]
+    for copy in copies:
+        copy.start()
+    slab_here, cross_user_here, cross_item_here, cross_two_here, hidden_here = copies
     left = iota((8, LANES), 1) < 64
     for t in range(user_width // LANES):
         for p in range(2):
@@ -100,6 +128,13 @@
         part = slice(k * devices, (k + 1) * devices)
         items_hot[part, :] = (row_lane == row_of[:, k : k + 1]).astype(BF)
         users_hot[part, :] = ((req_lane & 31) == req_of[:, k : k + 1]).astype(BF)
+    slab_here.wait()
+    for part in parts:
+        for cols in tiles(item_width):
+            first[part, user_width + cols.start : user_width + cols.stop] = jnp.dot(
+                items_hot[part, :], slab_ref[:, cols], preferred_element_type=F32
+            ).astype(BF)
+    cross_user_here.wait()
     base = jnp.dot(users_bf, cross_ref[0, :user_width, :], preferred_element_type=F32)
     base = base + (cross_bias_ref[0:1, :] + 1.0)
     base_high = base.astype(BF)
@@ -110,43 +145,47 @@
     shift[32:64, :] = base_mid
     shift[64:96, :] = base_low
     shift[96:128, :] = jnp.zeros_like(base_low)
-    first[:, :user_width] = jnp.dot(
-        users_hot[:, :32], users_bf, preferred_element_type=F32
-    ).astype(BF)
-    first[:, user_width:] = jnp.dot(
-        items_hot[...], slab_ref[...], preferred_element_type=F32
-    ).astype(BF)
-    tile = 1024
-
-    def layer_one(n, carry):
-        cols = pl.ds(pl.multiple_of(n * tile, tile), tile)
-        factor = jnp.dot(
-            first[:, user_width:], cross_ref[0, user_width:, cols], preferred_element_type=F32
-        )
-        factor += jnp.dot(users_hot[...], shift[:, cols], preferred_element_type=F32)
-        new = first[:, cols].astype(F32) * factor
-        state[:, cols] = new
-        state_bf[:, cols] = new.astype(BF)
-        return carry
-
-    lax.fori_loop(0, cross // tile, layer_one, 0)
-
-    def layer_two(n, carry):
-        cols = pl.ds(pl.multiple_of(n * tile, tile), tile)
-        mixed = jnp.dot(state_bf[...], cross_ref[1, :, cols], preferred_element_type=F32)
-        mixed += cross_bias_ref[1:2, cols]
-        state[:, cols] = first[:, cols].astype(F32) * mixed + state[:, cols]
-        return carry
-
-    lax.fori_loop(0, cross // tile, layer_two, 0)
-    state_bf[...] = state[...].astype(BF)
-    hidden = jnp.dot(state_bf[...], hidden_ref[...], preferred_element_type=F32)
-    hidden = jnp.maximum(hidden + hidden_bias_ref[...], 0.0).astype(BF)
-    logits[...] = jnp.dot(hidden, out_ref[...], preferred_element_type=F32)
+    for part in parts:
+        for cols in tiles(user_width):
+            first[part, cols] = jnp.dot(
+                users_hot[part, :32], users_bf[:, cols], preferred_element_type=F32
+            ).astype(BF)
+    cross_item_here.wait()
+    for part in parts:
+        for cols in tiles(cross):
+            factor = jnp.dot(
+                first[part, user_width:],
+                cross_ref[0, user_width:, cols],
+                preferred_element_type=F32,
+            )
+            factor += jnp.dot(users_hot[part, :], shift[:, cols], preferred_element_type=F32)
+            new = first[part, cols].astype(F32) * factor
+            state[part, cols] = new
+            state_one[part, cols] = new.astype(BF)
+    cross_two_here.wait()
+    for part in parts:
+        for cols in tiles(cross):
+            mixed = jnp.dot(
+                state_one[part, :], cross_ref[1, :, cols], preferred_element_type=F32
+            )
+            mixed += cross_bias_ref[1:2, cols]
+            new = first[part, cols].astype(F32) * mixed + state[part, cols]
+            state_two[part, cols] = new.astype(BF)
+    hidden_here.wait()
+    for part in parts:
+        for cols in tiles(hid):
+            got = jnp.dot(state_two[part, :], hidden_ref[:, cols], preferred_element_type=F32)
+            hidden[part, cols] = jnp.maximum(got + hidden_bias_ref[:, cols], 0.0).astype(BF)
+    out_rows = jnp.broadcast_to(out_ref[...], (LANES, hid))
     lane = iota((devices, LANES), 1)
     total = jnp.zeros((devices, LANES), F32)
-    for k in range(CAP):
-        total = jnp.where(lane == k, logits[k * devices : (k + 1) * devices, :], total)
+    for part in parts:
+        logits = lax.dot_general(
+            hidden[part, :], out_rows, (((1,), (1,)), ((), ())), preferred_element_type=F32
+        )
+        for k in range(half // devices):
+            here = lane == part.start // devices + k
+            total = jnp.where(here, logits[k * devices : (k + 1) * devices, :], total)
     score_ref[...] = jax.nn.sigmoid(total)
 
 
@@ -179,6 +218,7 @@
     cross = cross_weight.shape[1]
     hid = hidden_weight.shape[1]
     vmem = pl.BlockSpec(memory_space=pltpu.VMEM)
+    hbm = pl.BlockSpec(memory_space=pl.ANY)
     msg, key = pl.pallas_call(
         prepare_kernel,
         out_shape=(
@@ -190,13 +230,16 @@
         name="prepare",
     )(cand_ids, user_rows)
     asked = lax.all_to_all(msg, AXES, split_axis=0, concat_axis=0, tiled=True)
-    out_columns = jnp.broadcast_to(out_weight[:, None], (hid, LANES))
     scores = pl.pallas_call(
         score_kernel,
         out_shape=jax.ShapeDtypeStruct((devices, LANES), F32),
-        in_specs=[vmem] * 7,
+        in_specs=[vmem, hbm, hbm, vmem, hbm, vmem, vmem],
         out_specs=vmem,
         scratch_shapes=[
+            pltpu.VMEM(table_slab.shape, BF),
+            pltpu.VMEM(cross_weight.shape, BF),
+            pltpu.VMEM(hidden_weight.shape, BF),
+            pltpu.SemaphoreType.DMA((5,)),
             pltpu.VMEM((32, cross // 2), F32),
             pltpu.VMEM((LANES, cross), BF),
             pltpu.VMEM((slots, table_slab.shape[0]), BF),
@@ -204,9 +247,10 @@
             pltpu.VMEM((slots, cross), BF),
             pltpu.VMEM((slots, cross), F32),
             pltpu.VMEM((slots, cross), BF),
-            pltpu.VMEM((slots, LANES), F32),
+            pltpu.VMEM((slots, cross), BF),
+            pltpu.VMEM((slots, hid), BF),
         ],
-        compiler_params=pltpu.CompilerParams(vmem_limit_bytes=58 * 2**20),
+        compiler_params=pltpu.CompilerParams(vmem_limit_bytes=54 * 2**20),
         name="score",
     )(
         asked,
@@ -215,7 +259,7 @@
         cross_bias,
         hidden_weight,
         hidden_bias.reshape(1, hid),
-        out_columns,
+        out_weight.reshape(1, hid),
     )
     answered = lax.all_to_all(scores, AXES, split_axis=0, concat_axis=0, tiled=True)
     return pl.pallas_call(

time: 75.9 us -> 69.9 us (0.921)
  blocking collectives: 37.8 us -> 15.1 us
  starting transfers between devices: 0 us -> 11.5 us
  waiting for transfers between devices: 0 us -> 10.2 us
  Pallas kernels: 36.2 us -> 30.9 us
    all_to_all x1 -> x0, blocking collectives: 23.1 us -> none  [per_device(): asked = lax.all_to_all(msg, AXES, split_axis=0, concat_axis=0, tiled=True)]
    all_to_all x0 -> x1, starting transfers between devices: none -> 11.5 us  [per_device(): asked = lax.all_to_all(msg, AXES, split_axis=0, concat_axis=0, tiled=True)]
    all_to_all x0 -> x1, waiting for transfers between devices: none -> 10.2 us  [per_device(): asked = lax.all_to_all(msg, AXES, split_axis=0, concat_axis=0, tiled=True)]
    pallas_call x1, Pallas kernels: 32.1 us -> 26.9 us  [per_device(): pl.pallas_call(score_kernel, out_shape=jax.ShapeDtypeStruct((devices, LAN...]
    broadcast_in_dim x1 -> x0, local copies, waits for them, and re-layouts: 1.58 us -> none  [per_device(): out_columns = jnp.broadcast_to(out_weight[:, None], (hid, LANES))]
    reshape x0 -> x1, local copies, waits for them, and re-layouts: none -> 1.27 us  [per_device(): out_weight.reshape(1, hid)]
  transfers between devices with their start and end apart: 0 -> 1, of which waited for: 0 -> 1; matrix products, arithmetic and copies ran while one was open for 0% -> 2% of each run, Pallas kernels for 0% -> 0%
where the time goes in v2:
time: 69.9 us; the launch traced here: 69.7 us
  Pallas kernels  30.9 us (44%)
  blocking collectives  15.1 us (22%)
  starting transfers between devices  11.5 us (16%)
  waiting for transfers between devices  10.2 us (15%)
  local copies, waits for them, and re-layouts  1.96 us (3%)
    pallas_call x1, Pallas kernels, per_device(): pl.pallas_call(score_kernel, out_shape=jax.ShapeDtypeStruct((devices, LAN...  26.9 us
    all_to_all x1, blocking collectives, per_device(): lax.all_to_all(scores, AXES, split_axis=0, concat_axis=0, tiled=True)  15.1 us
    all_to_all x1, starting transfers between devices, per_device(): asked = lax.all_to_all(msg, AXES, split_axis=0, concat_axis=0, tiled=True)  11.5 us
    all_to_all x1, waiting for transfers between devices, per_device(): asked = lax.all_to_all(msg, AXES, split_axis=0, concat_axis=0, tiled=True)  10.2 us
    pallas_call x1, Pallas kernels, per_device(): pl.pallas_call(prepare_kernel, out_shape=(jax.ShapeDtypeStruct((devices *...  2.25 us
    pallas_call x1, Pallas kernels, per_device(): pl.pallas_call(collect_kernel, out_shape=jax.ShapeDtypeStruct((groups, wi...  1.79 us
  transfers between devices with their start and end apart: 1, of which 1 were waited for; matrix products, arithmetic and copies ran while one was open for 2% of the time, Pallas kernels for 0%

profile of v2, /device:TPU:1, one launch (start us, length us, event | category | flops | bytes accessed | tf_op | source)
XLA Modules:
  0.0 69.7 jit_solution(5456823519075363262)
XLA Ops:
  0.0 2.3 %prepare.1 = (f32[512,128]{1,0:T(8,128)}, s32[4,128]{1,0:T(4,128)}) custom-call(s32[4,128]{1,0:T(4,128)} %ids_ref.1, bf16[4,64]{1,0:T(4,128)(2,1)} %user_ref.1), custom_call_target="tpu_custom_call" | custom-call | tf_op jit(solution)/shard_map/prepare/pallas_call | solution.py:222
  2.3 11.5 %all-to-all-start = ((f32[128,4,128]{2,1,0:T(4,128)}), f32[128,4,128]{2,1,0:T(4,128)S(1)}, u32[]{:S(2)}, u32[]{:S(2)}) async-start(f32[128,4,128]{2,1,0:T(4,128)} %bitcast.9), calls=%async_computation | async-start | bytes 524288 | tf_op jit(solution)/shard_map/all_to_all | solution.py:232
  13.8 1.3 %reshape.11.out_ref = bf16[1,1024]{1,0:T(2,128)(2,1)} reshape(bf16[1024]{0:T(1024)(128)(2,1)} %param.15) | data formatting | bytes 4096 | tf_op jit(solution)/shard_map/reshape | solution.py:262
  15.0 10.2 %all-to-all-done = f32[128,4,128]{2,1,0:T(4,128)S(1)} async-done(((f32[128,4,128]{2,1,0:T(4,128)}), f32[128,4,128]{2,1,0:T(4,128)S(1)}, u32[]{:S(2)}, u32[]{:S(2)}) %all-to-all-start) | async-done | bytes 262176 | tf_op jit(solution)/shard_map/all_to_all | solution.py:232
  25.2 0.0 copy-start
  25.2 0.7 copy-done
  25.9 26.9 %score.1 = f32[128,128]{1,0:T(8,128)} custom-call(f32[512,128]{1,0:T(8,128)} %bitcast.7, bf16[1024,1024]{1,0:T(8,128)(2,1)} %slab_hbm.1, bf16[2,2048,2048]{2,1,0:T(8,128)(2,1)} %cross_hbm.1, f32[2,2048]{1,0:T(2,128)} %cross_bias_ref.1, bf16[2048,1024]{1,0:T(8,128)(2,1)} %hidden_hbm.1, f32[1,1024]{1,0:T(1,128)} %bitcast.11, bf16[1,1024]{1,0:T(2,128)(2,1)} %reshape.11.out_ref), custom_call_target="tpu_custom_call" | custom-call | tf_op jit(solution)/shard_map/score/pallas_call | solution.py:233
  52.8 15.1 %all_to_all.22 = f32[128,1,128]{2,1,0:T(1,128)} all-to-all(f32[128,1,128]{2,1,0:T(1,128)} %bitcast.8), channel_id=1, replica_groups=mesh['req'=8,'score'=16] {'req','score'}, dimensions={0} | all-to-all | bytes 131072 | tf_op jit(solution)/shard_map/all_to_all | solution.py:264
  67.9 1.8 %collect.1 = f32[4,128]{1,0:T(4,128)} custom-call(f32[128,128]{1,0:T(8,128)} %bitcast.10, s32[4,128]{1,0:T(4,128)} %get-tuple-element.8.key_ref), custom_call_target="tpu_custom_call" | custom-call | tf_op jit(solution)/shard_map/collect/pallas_call | solution.py:265
Async XLA Ops:
  2.3 22.9 %all-to-all-start = ((f32[128,4,128]{2,1,0:T(4,128)}), f32[128,4,128]{2,1,0:T(4,128)S(1)}, u32[]{:S(2)}, u32[]{:S(2)}) async-start(f32[128,4,128]{2,1,0:T(4,128)} %bitcast.9), calls=%async_computation | async-start | bytes 524288 | tf_op jit(solution)/shard_map/all_to_all | solution.py:232
  25.2 0.7 copy-start

commit v3 on v2

--- a/solution.py
+++ b/solution.py
@@ -17,7 +17,19 @@
     return lax.broadcasted_iota(jnp.int32, shape, axis)
 
 
-def prepare_kernel(ids_ref, user_ref, msg_ref, key_ref):
+def in_hbm(array):
+    return pltpu.with_memory_space_constraint(array, pltpu.HBM)
+
+
+def prepare_kernel(
+    ids_ref, user_ref, slab_hbm, cross_hbm, msg_ref, key_ref, slab_ref, cross_ref, wide, copied
+):
+    slab_here = pltpu.make_async_copy(slab_hbm, slab_ref, copied.at[0])
+    slab_here.start()
+    cross_here = pltpu.make_async_copy(
+        cross_hbm.at[0, pl.ds(0, cross_ref.shape[0])], cross_ref, copied.at[1]
+    )
+    cross_here.start()
     groups, width = ids_ref.shape
     devices = msg_ref.shape[0] // WORDS
     ids = ids_ref[...]
@@ -48,27 +60,30 @@
         jnp.concatenate([user[2 * p : 2 * p + 1, :], user[2 * p + 1 : 2 * p + 2, :]], axis=1)
         for p in range(2)
     ]
-    msg_ref[pl.ds(0, devices, stride=WORDS), :] = high * 16.0 + low
+    wide[pl.ds(0, devices, stride=WORDS), :] = high
     for p in range(2):
-        msg_ref[pl.ds(p + 1, devices, stride=WORDS), :] = jnp.broadcast_to(
-            pairs[p], (devices, LANES)
-        )
-    msg_ref[pl.ds(3, devices, stride=WORDS), :] = jnp.zeros((devices, LANES), F32)
+        wide[pl.ds(p + 1, devices, stride=WORDS), :] = jnp.broadcast_to(pairs[p], (devices, LANES))
+    wide[pl.ds(3, devices, stride=WORDS), :] = low
+    msg_ref[...] = wide[...].astype(BF)
+    slab_here.wait()
+    cross_here.wait()
 
 
 def score_kernel(
     msg_ref,
-    slab_hbm,
+    slab_ref,
+    cross_user_ref,
     cross_hbm,
     cross_bias_ref,
     hidden_hbm,
     hidden_bias_ref,
     out_ref,
     score_ref,
-    slab_ref,
-    cross_ref,
+    cross_item,
+    cross_two,
     hidden_ref,
     copied,
+    wide,
     users,
     shift,
     items_hot,
@@ -77,49 +92,49 @@
     state,
     state_one,
     state_two,
-    hidden,
 ):
     devices = msg_ref.shape[0] // WORDS
     rows = slab_ref.shape[0]
     item_width = slab_ref.shape[1]
-    cross = cross_ref.shape[1]
+    cross = cross_item.shape[1]
     user_width = cross - item_width
     hid = hidden_ref.shape[1]
     slots = CAP * devices
     per_req = devices // 8
-    half = 512
+    half = slots // 2
+    half_ranks = CAP // 2
     tile = 512
     parts = [slice(h, h + half) for h in range(0, slots, half)]
 
     def tiles(width):
         return [slice(n, n + tile) for n in range(0, width, tile)]
 
-    lower, upper = pl.ds(0, user_width), pl.ds(user_width, item_width)
     copies = [
         pltpu.make_async_copy(source, target, copied.at[i])
         for i, (source, target) in enumerate(
             [
-                (slab_hbm, slab_ref),
-                (cross_hbm.at[0, lower], cross_ref.at[0, lower]),
-                (cross_hbm.at[0, upper], cross_ref.at[0, upper]),
-                (cross_hbm.at[1], cross_ref.at[1]),
+                (cross_hbm.at[0, pl.ds(user_width, item_width)], cross_item),
+                (cross_hbm.at[1], cross_two),
                 (hidden_hbm, hidden_ref),
             ]
         )
     ]
     for copy in copies:
         copy.start()
-    slab_here, cross_user_here, cross_item_here, cross_two_here, hidden_here = copies
+    cross_item_here, cross_two_here, hidden_here = copies
+    wide[...] = msg_ref[...].astype(F32)
     left = iota((8, LANES), 1) < 64
     for t in range(user_width // LANES):
         for p in range(2):
-            even = msg_ref[pl.ds(8 * t + 1 + p, 8, stride=WORDS * per_req), :]
-            odd = msg_ref[pl.ds(8 * t + 5 + p, 8, stride=WORDS * per_req), :]
+            even = wide[pl.ds(8 * t + 1 + p, 8, stride=WORDS * per_req), :]
+            odd = wide[pl.ds(8 * t + 5 + p, 8, stride=WORDS * per_req), :]
             cols = slice(t * LANES, (t + 1) * LANES)
             users[16 * p : 16 * p + 8, cols] = jnp.where(left, even, pltpu.roll(odd, 64, 1))
             users[16 * p + 8 : 16 * p + 16, cols] = jnp.where(left, pltpu.roll(even, 64, 1), odd)
     users_bf = users[...].astype(BF)
-    value = msg_ref[pl.ds(0, devices, stride=WORDS), :].astype(jnp.int32) - 1
+    value = wide[pl.ds(0, devices, stride=WORDS), :] * 16.0
+    value += wide[pl.ds(3, devices, stride=WORDS), :]
+    value = value.astype(jnp.int32) - 1
     row_of = value >> 2
     req_of = (value & 3) * 8 + iota((devices, LANES), 0) // per_req
     row_lane = iota((devices, rows), 1)
@@ -128,14 +143,12 @@
         part = slice(k * devices, (k + 1) * devices)
         items_hot[part, :] = (row_lane == row_of[:, k : k + 1]).astype(BF)
         users_hot[part, :] = ((req_lane & 31) == req_of[:, k : k + 1]).astype(BF)
-    slab_here.wait()
     for part in parts:
         for cols in tiles(item_width):
             first[part, user_width + cols.start : user_width + cols.stop] = jnp.dot(
                 items_hot[part, :], slab_ref[:, cols], preferred_element_type=F32
             ).astype(BF)
-    cross_user_here.wait()
-    base = jnp.dot(users_bf, cross_ref[0, :user_width, :], preferred_element_type=F32)
+    base = jnp.dot(users_bf, cross_user_ref[...], preferred_element_type=F32)
     base = base + (cross_bias_ref[0:1, :] + 1.0)
     base_high = base.astype(BF)
     rest = base - base_high.astype(F32)
@@ -155,7 +168,7 @@
         for cols in tiles(cross):
             factor = jnp.dot(
                 first[part, user_width:],
-                cross_ref[0, user_width:, cols],
+                cross_item[:, cols],
                 preferred_element_type=F32,
             )
             factor += jnp.dot(users_hot[part, :], shift[:, cols], preferred_element_type=F32)
@@ -166,26 +179,32 @@
     for part in parts:
         for cols in tiles(cross):
             mixed = jnp.dot(
-                state_one[part, :], cross_ref[1, :, cols], preferred_element_type=F32
+                state_one[part, :], cross_two[:, cols], preferred_element_type=F32
             )
             mixed += cross_bias_ref[1:2, cols]
             new = first[part, cols].astype(F32) * mixed + state[part, cols]
             state_two[part, cols] = new.astype(BF)
     hidden_here.wait()
-    for part in parts:
-        for cols in tiles(hid):
-            got = jnp.dot(state_two[part, :], hidden_ref[:, cols], preferred_element_type=F32)
-            hidden[part, cols] = jnp.maximum(got + hidden_bias_ref[:, cols], 0.0).astype(BF)
-    out_rows = jnp.broadcast_to(out_ref[...], (LANES, hid))
     lane = iota((devices, LANES), 1)
     total = jnp.zeros((devices, LANES), F32)
-    for part in parts:
-        logits = lax.dot_general(
-            hidden[part, :], out_rows, (((1,), (1,)), ((), ())), preferred_element_type=F32
-        )
-        for k in range(half // devices):
-            here = lane == part.start // devices + k
-            total = jnp.where(here, logits[k * devices : (k + 1) * devices, :], total)
+    for part in range(2):
+        gathered = jnp.zeros((half, LANES), F32)
+        for start in range(0, hid, tile):
+            cols = slice(start, start + tile)
+            hidden = jnp.dot(
+                state_two[part * half : (part + 1) * half, :],
+                hidden_ref[:, cols],
+                preferred_element_type=F32,
+            )
+            for j in range(tile // LANES):
+                at = start // LANES + j
+                unit = hidden[:, j * LANES : (j + 1) * LANES] + hidden_bias_ref[at : at + 1, :]
+                unit = jnp.maximum(unit, 0.0).astype(BF).astype(F32)
+                gathered += unit * out_ref[at : at + 1, :].astype(F32)
+        logit = jnp.sum(gathered, axis=1, keepdims=True)
+        for k in range(half_ranks):
+            here = lane == part * half_ranks + k
+            total = jnp.where(here, logit[k * devices : (k + 1) * devices, :], total)
     score_ref[...] = jax.nn.sigmoid(total)
 
 
@@ -219,28 +238,39 @@
     hid = hidden_weight.shape[1]
     vmem = pl.BlockSpec(memory_space=pltpu.VMEM)
     hbm = pl.BlockSpec(memory_space=pl.ANY)
-    msg, key = pl.pallas_call(
+    item_width = table_slab.shape[1]
+    user_width = cross - item_width
+    in_vmem = pltpu.with_memory_space_constraint
+    msg, key, slab, cross_user = pl.pallas_call(
         prepare_kernel,
         out_shape=(
-            jax.ShapeDtypeStruct((devices * WORDS, LANES), F32),
+            jax.ShapeDtypeStruct((devices * WORDS, LANES), BF),
             jax.ShapeDtypeStruct((groups, width), jnp.int32),
+            pltpu.VMEM(table_slab.shape, BF),
+            pltpu.VMEM((user_width, cross), BF),
         ),
-        in_specs=[vmem, vmem],
-        out_specs=(vmem, vmem),
+        in_specs=[vmem, vmem, hbm, hbm],
+        out_specs=(vmem, vmem, vmem, vmem),
+        scratch_shapes=[
+            pltpu.VMEM((devices * WORDS, LANES), F32),
+            pltpu.SemaphoreType.DMA((2,)),
+        ],
+        compiler_params=pltpu.CompilerParams(vmem_limit_bytes=16 * 2**20),
         name="prepare",
-    )(cand_ids, user_rows)
+    )(in_hbm(cand_ids), in_hbm(user_rows), in_hbm(table_slab), in_hbm(cross_weight))
     asked = lax.all_to_all(msg, AXES, split_axis=0, concat_axis=0, tiled=True)
     scores = pl.pallas_call(
         score_kernel,
-        out_shape=jax.ShapeDtypeStruct((devices, LANES), F32),
-        in_specs=[vmem, hbm, hbm, vmem, hbm, vmem, vmem],
+        out_shape=pltpu.VMEM((devices, LANES), F32),
+        in_specs=[vmem, vmem, vmem, hbm, vmem, hbm, vmem, vmem],
         out_specs=vmem,
         scratch_shapes=[
-            pltpu.VMEM(table_slab.shape, BF),
-            pltpu.VMEM(cross_weight.shape, BF),
-            pltpu.VMEM(hidden_weight.shape, BF),
-            pltpu.SemaphoreType.DMA((5,)),
-            pltpu.VMEM((32, cross // 2), F32),
+            pltpu.VMEM((item_width, cross), BF),
+            pltpu.VMEM((cross, cross), BF),
+            pltpu.VMEM((cross, hid), BF),
+            pltpu.SemaphoreType.DMA((3,)),
+            pltpu.VMEM((devices * WORDS, LANES), F32),
+            pltpu.VMEM((32, user_width), F32),
             pltpu.VMEM((LANES, cross), BF),
             pltpu.VMEM((slots, table_slab.shape[0]), BF),
             pltpu.VMEM((slots, LANES), BF),
@@ -248,18 +278,18 @@
             pltpu.VMEM((slots, cross), F32),
             pltpu.VMEM((slots, cross), BF),
             pltpu.VMEM((slots, cross), BF),
-            pltpu.VMEM((slots, hid), BF),
         ],
-        compiler_params=pltpu.CompilerParams(vmem_limit_bytes=54 * 2**20),
+        compiler_params=pltpu.CompilerParams(vmem_limit_bytes=50 * 2**20),
         name="score",
     )(
         asked,
-        table_slab,
-        cross_weight,
+        in_vmem(slab, pltpu.VMEM),
+        in_vmem(cross_user, pltpu.VMEM),
+        in_hbm(cross_weight),
         cross_bias,
-        hidden_weight,
-        hidden_bias.reshape(1, hid),
-        out_weight.reshape(1, hid),
+        in_hbm(hidden_weight),
+        hidden_bias.reshape(hid // LANES, LANES),
+        out_weight.reshape(hid // LANES, LANES),
     )
     answered = lax.all_to_all(scores, AXES, split_axis=0, concat_axis=0, tiled=True)
     return pl.pallas_call(

time: 69.9 us -> 65.7 us (0.940)
  blocking collectives: 15.1 us -> 35.9 us
  starting transfers between devices: 11.5 us -> 0 us
  waiting for transfers between devices: 10.2 us -> 0 us
  local copies, waits for them, and re-layouts: 1.96 us -> 0.01 us
  Pallas kernels: 30.9 us -> 29.5 us
    all_to_all x0 -> x1, blocking collectives: none -> 21.9 us  [per_device(): asked = lax.all_to_all(msg, AXES, split_axis=0, concat_axis=0, tiled=True)]
    all_to_all x1 -> x0, starting transfers between devices: 11.5 us -> none  [per_device(): asked = lax.all_to_all(msg, AXES, split_axis=0, concat_axis=0, tiled=True)]
    all_to_all x1 -> x0, waiting for transfers between devices: 10.2 us -> none  [per_device(): asked = lax.all_to_all(msg, AXES, split_axis=0, concat_axis=0, tiled=True)]
    pallas_call x1, Pallas kernels: 26.9 us -> 24.1 us  [per_device(): pl.pallas_call(score_kernel, out_shape=pltpu.VMEM((devices, LANES), F32),...]
    pallas_call x1, Pallas kernels: 2.25 us -> 3.54 us  [per_device(): pl.pallas_call(prepare_kernel, out_shape=(jax.ShapeDtypeStruct((devices *...]
    reshape x1 -> x0, local copies, waits for them, and re-layouts: 1.27 us -> none  [per_device(): out_weight.reshape(1, hid)]
    all_to_all x1, blocking collectives: 15.1 us -> 14 us  [per_device(): lax.all_to_all(scores, AXES, split_axis=0, concat_axis=0, tiled=True)]
  transfers between devices with their start and end apart: 1 -> 0, of which waited for: 1 -> 0; matrix products, arithmetic and copies ran while one was open for 2% -> 0% of each run, Pallas kernels for 0% -> 0%
where the time goes in v3:
time: 65.7 us; the launch traced here: 65.4 us
  blocking collectives  35.9 us (55%)
  Pallas kernels  29.5 us (45%)
    pallas_call x1, Pallas kernels, per_device(): pl.pallas_call(score_kernel, out_shape=pltpu.VMEM((devices, LANES), F32),...  24.1 us
    all_to_all x1, blocking collectives, per_device(): asked = lax.all_to_all(msg, AXES, split_axis=0, concat_axis=0, tiled=True)  21.9 us
    all_to_all x1, blocking collectives, per_device(): lax.all_to_all(scores, AXES, split_axis=0, concat_axis=0, tiled=True)  14 us
    pallas_call x1, Pallas kernels, per_device(): pl.pallas_call(prepare_kernel, out_shape=(jax.ShapeDtypeStruct((devices *...  3.54 us
    pallas_call x1, Pallas kernels, per_device(): pl.pallas_call(collect_kernel, out_shape=jax.ShapeDtypeStruct((groups, wi...  1.79 us

profile of v3, /device:TPU:1, one launch (start us, length us, event | category | flops | bytes accessed | tf_op | source)
XLA Modules:
  0.0 65.4 jit_solution(18361907547606868955)
XLA Ops:
  0.0 3.5 %prepare.1 = (bf16[512,128]{1,0:T(8,128)(2,1)S(1)}, s32[4,128]{1,0:T(4,128)S(1)}, bf16[1024,1024]{1,0:T(8,128)(2,1)S(1)}, bf16[1024,2048]{1,0:T(8,128)(2,1)S(1)}) custom-call(s32[4,128]{1,0:T(4,128)} %ids_ref.1, bf16[4,64]{1,0:T(4,128)(2,1)} %user_ref.1, bf16[1024,1024]{1,0:T(8,128)(2,1)} %slab_hbm.1, bf16[2,2048,2048]{2,1,0:T(8,128)(2,1)} %cross_hbm.3), custom_call_target="tpu_custom_call" | custom-call | tf_op jit(solution)/shard_map/prepare/pallas_call | solution.py:244
  3.5 0.0 copy-start
  3.6 21.9 %all_to_all.22 = bf16[128,4,128]{2,1,0:T(4,128)(2,1)} all-to-all(bf16[128,4,128]{2,1,0:T(4,128)(2,1)S(1)} %bitcast.9), channel_id=1, replica_groups=mesh['req'=8,'score'=16] {'req','score'}, dimensions={0} | all-to-all | bytes 262144 | tf_op jit(solution)/shard_map/all_to_all | solution.py:261
  25.5 0.0 copy-done
  25.5 24.1 %score.1 = f32[128,128]{1,0:T(8,128)S(1)} custom-call(bf16[512,128]{1,0:T(8,128)(2,1)} %bitcast.10, bf16[1024,1024]{1,0:T(8,128)(2,1)S(1)} %get-tuple-element.10.slab_ref, bf16[1024,2048]{1,0:T(8,128)(2,1)S(1)} %get-tuple-element.11.cross_user_ref, bf16[2,2048,2048]{2,1,0:T(8,128)(2,1)} %cross_hbm.3, f32[2,2048]{1,0:T(2,128)} %cross_bias_ref.1, ...), custom_call_target="tpu_custom_call" | custom-call | tf_op jit(solution)/shard_map/score/pallas_call | solution.py:262
  49.6 14.0 %all_to_all.23 = f32[128,1,128]{2,1,0:T(1,128)} all-to-all(f32[128,1,128]{2,1,0:T(1,128)S(1)} %bitcast.8), channel_id=1, replica_groups=mesh['req'=8,'score'=16] {'req','score'}, dimensions={0} | all-to-all | bytes 131072 | tf_op jit(solution)/shard_map/all_to_all | solution.py:294
  63.6 1.8 %collect.1 = f32[4,128]{1,0:T(4,128)} custom-call(f32[128,128]{1,0:T(8,128)} %bitcast.11, s32[4,128]{1,0:T(4,128)} %copy-done), custom_call_target="tpu_custom_call" | custom-call | tf_op jit(solution)/shard_map/collect/pallas_call | solution.py:295
Async XLA Ops:
  3.5 21.9 %copy-start = (s32[4,128]{1,0:T(4,128)}, s32[4,128]{1,0:T(4,128)S(1)}, u32[]{:S(2)}) copy-start(s32[4,128]{1,0:T(4,128)S(1)} %get-tuple-element.12.key_ref) | copy-start | bytes 6148

commit v4 on v3

--- a/solution.py
+++ b/solution.py
@@ -22,14 +22,12 @@
 
 
 def prepare_kernel(
-    ids_ref, user_ref, slab_hbm, cross_hbm, msg_ref, key_ref, slab_ref, cross_ref, wide, copied
+    ids_ref, user_ref, slab_hbm, msg_ref, key_ref, slab_ref, wide, copied
 ):
-    slab_here = pltpu.make_async_copy(slab_hbm, slab_ref, copied.at[0])
+    slab_here = pltpu.make_async_copy(
+        slab_hbm.at[:, pl.ds(0, slab_ref.shape[1])], slab_ref, copied
+    )
     slab_here.start()
-    cross_here = pltpu.make_async_copy(
-        cross_hbm.at[0, pl.ds(0, cross_ref.shape[0])], cross_ref, copied.at[1]
-    )
-    cross_here.start()
     groups, width = ids_ref.shape
     devices = msg_ref.shape[0] // WORDS
     ids = ids_ref[...]
@@ -66,19 +64,20 @@
     wide[pl.ds(3, devices, stride=WORDS), :] = low
     msg_ref[...] = wide[...].astype(BF)
     slab_here.wait()
-    cross_here.wait()
 
 
 def score_kernel(
     msg_ref,
     slab_ref,
-    cross_user_ref,
+    slab_hbm,
     cross_hbm,
     cross_bias_ref,
     hidden_hbm,
     hidden_bias_ref,
     out_ref,
     score_ref,
+    slab_rest,
+    cross_user,
     cross_item,
     cross_two,
     hidden_ref,
@@ -95,7 +94,8 @@
 ):
     devices = msg_ref.shape[0] // WORDS
     rows = slab_ref.shape[0]
-    item_width = slab_ref.shape[1]
+    staged = slab_ref.shape[1]
+    item_width = staged + slab_rest.shape[1]
     cross = cross_item.shape[1]
     user_width = cross - item_width
     hid = hidden_ref.shape[1]
@@ -113,6 +113,8 @@
         pltpu.make_async_copy(source, target, copied.at[i])
         for i, (source, target) in enumerate(
             [
+                (slab_hbm.at[:, pl.ds(staged, item_width - staged)], slab_rest),
+                (cross_hbm.at[0, pl.ds(0, user_width)], cross_user),
                 (cross_hbm.at[0, pl.ds(user_width, item_width)], cross_item),
                 (cross_hbm.at[1], cross_two),
                 (hidden_hbm, hidden_ref),
@@ -121,7 +123,7 @@
     ]
     for copy in copies:
         copy.start()
-    cross_item_here, cross_two_here, hidden_here = copies
+    slab_here, cross_user_here, cross_item_here, cross_two_here, hidden_here = copies
     wide[...] = msg_ref[...].astype(F32)
     left = iota((8, LANES), 1) < 64
     for t in range(user_width // LANES):
@@ -143,12 +145,16 @@
         part = slice(k * devices, (k + 1) * devices)
         items_hot[part, :] = (row_lane == row_of[:, k : k + 1]).astype(BF)
         users_hot[part, :] = ((req_lane & 31) == req_of[:, k : k + 1]).astype(BF)
-    for part in parts:
-        for cols in tiles(item_width):
-            first[part, user_width + cols.start : user_width + cols.stop] = jnp.dot(
-                items_hot[part, :], slab_ref[:, cols], preferred_element_type=F32
-            ).astype(BF)
-    base = jnp.dot(users_bf, cross_user_ref[...], preferred_element_type=F32)
+    for table, at in ((slab_ref, user_width), (slab_rest, user_width + staged)):
+        if table is slab_rest:
+            slab_here.wait()
+        for part in parts:
+            for cols in tiles(table.shape[1]):
+                first[part, at + cols.start : at + cols.stop] = jnp.dot(
+                    items_hot[part, :], table[:, cols], preferred_element_type=F32
+                ).astype(BF)
+    cross_user_here.wait()
+    base = jnp.dot(users_bf, cross_user[...], preferred_element_type=F32)
     base = base + (cross_bias_ref[0:1, :] + 1.0)
     base_high = base.astype(BF)
     rest = base - base_high.astype(F32)
@@ -241,34 +247,36 @@
     item_width = table_slab.shape[1]
     user_width = cross - item_width
     in_vmem = pltpu.with_memory_space_constraint
-    msg, key, slab, cross_user = pl.pallas_call(
+    staged = item_width // 2
+    msg, key, slab = pl.pallas_call(
         prepare_kernel,
         out_shape=(
             jax.ShapeDtypeStruct((devices * WORDS, LANES), BF),
             jax.ShapeDtypeStruct((groups, width), jnp.int32),
-            pltpu.VMEM(table_slab.shape, BF),
-            pltpu.VMEM((user_width, cross), BF),
+            pltpu.VMEM((table_slab.shape[0], staged), BF),
         ),
-        in_specs=[vmem, vmem, hbm, hbm],
-        out_specs=(vmem, vmem, vmem, vmem),
+        in_specs=[vmem, vmem, hbm],
+        out_specs=(vmem, vmem, vmem),
         scratch_shapes=[
             pltpu.VMEM((devices * WORDS, LANES), F32),
-            pltpu.SemaphoreType.DMA((2,)),
+            pltpu.SemaphoreType.DMA,
         ],
         compiler_params=pltpu.CompilerParams(vmem_limit_bytes=16 * 2**20),
         name="prepare",
-    )(in_hbm(cand_ids), in_hbm(user_rows), in_hbm(table_slab), in_hbm(cross_weight))
+    )(in_hbm(cand_ids), in_hbm(user_rows), in_hbm(table_slab))
     asked = lax.all_to_all(msg, AXES, split_axis=0, concat_axis=0, tiled=True)
     scores = pl.pallas_call(
         score_kernel,
         out_shape=pltpu.VMEM((devices, LANES), F32),
-        in_specs=[vmem, vmem, vmem, hbm, vmem, hbm, vmem, vmem],
+        in_specs=[vmem, vmem, hbm, hbm, vmem, hbm, vmem, vmem],
         out_specs=vmem,
         scratch_shapes=[
+            pltpu.VMEM((table_slab.shape[0], item_width - staged), BF),
+            pltpu.VMEM((user_width, cross), BF),
             pltpu.VMEM((item_width, cross), BF),
             pltpu.VMEM((cross, cross), BF),
             pltpu.VMEM((cross, hid), BF),
-            pltpu.SemaphoreType.DMA((3,)),
+            pltpu.SemaphoreType.DMA((5,)),
             pltpu.VMEM((devices * WORDS, LANES), F32),
             pltpu.VMEM((32, user_width), F32),
             pltpu.VMEM((LANES, cross), BF),
@@ -284,12 +292,12 @@
     )(
         asked,
         in_vmem(slab, pltpu.VMEM),
-        in_vmem(cross_user, pltpu.VMEM),
+        in_hbm(table_slab),
         in_hbm(cross_weight),
-        cross_bias,
+        in_hbm(cross_bias),
         in_hbm(hidden_weight),
-        hidden_bias.reshape(hid // LANES, LANES),
-        out_weight.reshape(hid // LANES, LANES),
+        in_hbm(hidden_bias.reshape(hid // LANES, LANES)),
+        in_hbm(out_weight.reshape(hid // LANES, LANES)),
     )
     answered = lax.all_to_all(scores, AXES, split_axis=0, concat_axis=0, tiled=True)
     return pl.pallas_call(
@@ -297,6 +305,7 @@
         out_shape=jax.ShapeDtypeStruct((groups, width), F32),
         in_specs=[vmem, vmem],
         out_specs=vmem,
+        compiler_params=pltpu.CompilerParams(vmem_limit_bytes=2 * 2**20),
         name="collect",
     )(answered, key)
 

time: 65.7 us -> 62.7 us (0.954)
  Pallas kernels: 29.5 us -> 27.2 us
    pallas_call x1, Pallas kernels: 3.54 us -> 1.93 us  [per_device(): pl.pallas_call(prepare_kernel, out_shape=(jax.ShapeDtypeStruct((devices *...]
    pallas_call x1, Pallas kernels: 1.79 us -> 0.95 us  [per_device(): pl.pallas_call(collect_kernel, out_shape=jax.ShapeDtypeStruct((groups, wi...]
where the time goes in v4:
time: 62.7 us; the launch traced here: 62.4 us
  blocking collectives  35.3 us (56%)
  Pallas kernels  27.2 us (43%)
    pallas_call x1, Pallas kernels, per_device(): pl.pallas_call(score_kernel, out_shape=pltpu.VMEM((devices, LANES), F32),...  24.3 us
    all_to_all x1, blocking collectives, per_device(): asked = lax.all_to_all(msg, AXES, split_axis=0, concat_axis=0, tiled=True)  21.7 us
    all_to_all x1, blocking collectives, per_device(): lax.all_to_all(scores, AXES, split_axis=0, concat_axis=0, tiled=True)  13.6 us
    pallas_call x1, Pallas kernels, per_device(): pl.pallas_call(prepare_kernel, out_shape=(jax.ShapeDtypeStruct((devices *...  1.93 us

profile of v4, /device:TPU:1, one launch (start us, length us, event | category | flops | bytes accessed | tf_op | source)
XLA Modules:
  0.0 62.4 jit_solution(5157001888924300825)
XLA Ops:
  0.0 1.9 %prepare.1 = (bf16[512,128]{1,0:T(8,128)(2,1)S(1)}, s32[4,128]{1,0:T(4,128)S(1)}, bf16[1024,512]{1,0:T(8,128)(2,1)S(1)}) custom-call(s32[4,128]{1,0:T(4,128)} %ids_ref.1, bf16[4,64]{1,0:T(4,128)(2,1)} %user_ref.1, bf16[1024,1024]{1,0:T(8,128)(2,1)} %slab_hbm.3), custom_call_target="tpu_custom_call" | custom-call | tf_op jit(solution)/shard_map/prepare/pallas_call | solution.py:251
  1.9 21.7 %all_to_all.22 = bf16[128,4,128]{2,1,0:T(4,128)(2,1)S(1)} all-to-all(bf16[128,4,128]{2,1,0:T(4,128)(2,1)S(1)} %bitcast.11), channel_id=1, replica_groups=mesh['req'=8,'score'=16] {'req','score'}, dimensions={0} | all-to-all | bytes 262144 | tf_op jit(solution)/shard_map/all_to_all | solution.py:267
  23.6 24.3 %score.1 = f32[128,128]{1,0:T(8,128)S(1)} custom-call(bf16[512,128]{1,0:T(8,128)(2,1)S(1)} %bitcast.8, bf16[1024,512]{1,0:T(8,128)(2,1)S(1)} %get-tuple-element.9.slab_ref, bf16[1024,1024]{1,0:T(8,128)(2,1)} %slab_hbm.3, bf16[2,2048,2048]{2,1,0:T(8,128)(2,1)} %cross_hbm.1, f32[2,2048]{1,0:T(2,128)} %cross_bias_ref.1, bf16[2048,1024]{1,0:T(8,128)(2,1)} %hidden_hbm.1, ...), custom_call_target="tpu_custom_call" | custom-call | tf_op jit(solution)/shard_map/score/pallas_call | solution.py:268
  47.9 13.6 %all_to_all.23 = f32[128,1,128]{2,1,0:T(1,128)S(1)} all-to-all(f32[128,1,128]{2,1,0:T(1,128)S(1)} %bitcast.9), channel_id=1, replica_groups=mesh['req'=8,'score'=16] {'req','score'}, dimensions={0} | all-to-all | bytes 131072 | tf_op jit(solution)/shard_map/all_to_all | solution.py:302
  61.5 1.0 %collect.1 = f32[4,128]{1,0:T(4,128)} custom-call(f32[128,128]{1,0:T(8,128)S(1)} %bitcast.10, s32[4,128]{1,0:T(4,128)S(1)} %get-tuple-element.10.key_ref), custom_call_target="tpu_custom_call" | custom-call | tf_op jit(solution)/shard_map/collect/pallas_call | solution.py:303

commit v5 on v4

--- a/solution.py
+++ b/solution.py
@@ -85,8 +85,8 @@
     wide,
     users,
     shift,
+    request,
     items_hot,
-    users_hot,
     first,
     state,
     state_one,
@@ -109,88 +109,135 @@
     def tiles(width):
         return [slice(n, n + tile) for n in range(0, width, tile)]
 
-    copies = [
-        pltpu.make_async_copy(source, target, copied.at[i])
-        for i, (source, target) in enumerate(
-            [
-                (slab_hbm.at[:, pl.ds(staged, item_width - staged)], slab_rest),
-                (cross_hbm.at[0, pl.ds(0, user_width)], cross_user),
-                (cross_hbm.at[0, pl.ds(user_width, item_width)], cross_item),
-                (cross_hbm.at[1], cross_two),
-                (hidden_hbm, hidden_ref),
-            ]
+    def copy(i, source, target):
+        return pltpu.make_async_copy(source, target, copied.at[i])
+
+    columns = tiles(cross)
+    count = len(columns)
+    slab_here = copy(0, slab_hbm.at[:, pl.ds(staged, item_width - staged)], slab_rest)
+    cross_two_here = copy(1, cross_hbm.at[1], cross_two)
+    hidden_here = copy(2, hidden_hbm, hidden_ref)
+    user_here, item_here = [], []
+    for n, cols in enumerate(columns):
+        cols = pl.ds(cols.start, tile)
+        user_here.append(
+            copy(3 + n, cross_hbm.at[0, pl.ds(0, user_width), cols], cross_user.at[:, cols])
         )
-    ]
-    for copy in copies:
-        copy.start()
-    slab_here, cross_user_here, cross_item_here, cross_two_here, hidden_here = copies
+        item_here.append(
+            copy(
+                3 + count + n,
+                cross_hbm.at[0, pl.ds(user_width, item_width), cols],
+                cross_item.at[:, cols],
+            )
+        )
+    slab_here.start()
+    for n in range(count):
+        user_here[n].start()
+        item_here[n].start()
     wide[...] = msg_ref[...].astype(F32)
+
+    def fetch(part, table, at):
+        for cols in tiles(table.shape[1]):
+            first[part, at + cols.start : at + cols.stop] = jnp.dot(
+                items_hot[part, :], table[:, cols], preferred_element_type=F32
+            ).astype(BF)
+
+    value = wide[pl.ds(0, devices, stride=WORDS), :] * 16.0
+    value += wide[pl.ds(3, devices, stride=WORDS), :]
+    value = value.astype(jnp.int32) - 1
+    row_of = value >> 2
+    req_of = (value & 3) + (iota((devices, LANES), 0) // per_req & 1) * 4
+    row_lane = iota((devices, rows), 1)
+    for part in parts:
+        for k in range(part.start // devices, part.stop // devices):
+            here = slice(k * devices, (k + 1) * devices)
+            items_hot[here, :] = (row_lane == row_of[:, k : k + 1]).astype(BF)
+            request[here, :] = jnp.broadcast_to(req_of[:, k : k + 1], (devices, LANES))
+        fetch(part, slab_ref, user_width)
     left = iota((8, LANES), 1) < 64
     for t in range(user_width // LANES):
         for p in range(2):
             even = wide[pl.ds(8 * t + 1 + p, 8, stride=WORDS * per_req), :]
             odd = wide[pl.ds(8 * t + 5 + p, 8, stride=WORDS * per_req), :]
-            cols = slice(t * LANES, (t + 1) * LANES)
-            users[16 * p : 16 * p + 8, cols] = jnp.where(left, even, pltpu.roll(odd, 64, 1))
-            users[16 * p + 8 : 16 * p + 16, cols] = jnp.where(left, pltpu.roll(even, 64, 1), odd)
-    users_bf = users[...].astype(BF)
-    value = wide[pl.ds(0, devices, stride=WORDS), :] * 16.0
-    value += wide[pl.ds(3, devices, stride=WORDS), :]
-    value = value.astype(jnp.int32) - 1
-    row_of = value >> 2
-    req_of = (value & 3) * 8 + iota((devices, LANES), 0) // per_req
-    row_lane = iota((devices, rows), 1)
-    req_lane = iota((devices, LANES), 1)
-    for k in range(CAP):
-        part = slice(k * devices, (k + 1) * devices)
-        items_hot[part, :] = (row_lane == row_of[:, k : k + 1]).astype(BF)
-        users_hot[part, :] = ((req_lane & 31) == req_of[:, k : k + 1]).astype(BF)
-    for table, at in ((slab_ref, user_width), (slab_rest, user_width + staged)):
-        if table is slab_rest:
-            slab_here.wait()
-        for part in parts:
-            for cols in tiles(table.shape[1]):
-                first[part, at + cols.start : at + cols.stop] = jnp.dot(
-                    items_hot[part, :], table[:, cols], preferred_element_type=F32
-                ).astype(BF)
-    cross_user_here.wait()
-    base = jnp.dot(users_bf, cross_user[...], preferred_element_type=F32)
-    base = base + (cross_bias_ref[0:1, :] + 1.0)
-    base_high = base.astype(BF)
-    rest = base - base_high.astype(F32)
-    base_mid = rest.astype(BF)
-    base_low = (rest - base_mid.astype(F32)).astype(BF)
-    shift[0:32, :] = base_high
-    shift[32:64, :] = base_mid
-    shift[64:96, :] = base_low
-    shift[96:128, :] = jnp.zeros_like(base_low)
+            users[t, pl.ds(2 * p, 8, stride=4), :] = jnp.where(left, even, pltpu.roll(odd, 64, 1))
+            users[t, pl.ds(2 * p + 1, 8, stride=4), :] = jnp.where(
+                left, pltpu.roll(even, 64, 1), odd
+            )
+    slab_here.wait()
     for part in parts:
-        for cols in tiles(user_width):
-            first[part, cols] = jnp.dot(
-                users_hot[part, :32], users_bf[:, cols], preferred_element_type=F32
-            ).astype(BF)
-    cross_item_here.wait()
+        fetch(part, slab_rest, user_width + staged)
+    users_bf = jnp.concatenate(
+        [users[t].astype(BF) for t in range(user_width // LANES)], axis=1
+    )
+    along_rows = lax.GatherDimensionNumbers(
+        offset_dims=(),
+        collapsed_slice_dims=(0,),
+        start_index_map=(0,),
+        operand_batching_dims=(1,),
+        start_indices_batching_dims=(1,),
+    )
+
+    def of_request(rows, places):
+        got = [
+            lax.gather(
+                rows,
+                place,
+                along_rows,
+                slice_sizes=(1, 1),
+                mode=lax.GatherScatterMode.PROMISE_IN_BOUNDS,
+            )
+            for place in places
+        ]
+        return jnp.concatenate(got, axis=0)
+
+    def request_term(n):
+        user_here[n].wait()
+        item_here[n].wait()
+        cols = columns[n]
+        base = jnp.dot(users_bf, cross_user[:, cols], preferred_element_type=F32)
+        shift[:, cols] = base + (cross_bias_ref[0:1, cols] + 1.0)
+
+    def layer_one(part, cols):
+        mixed = jnp.dot(first[part, user_width:], cross_item[:, cols], preferred_element_type=F32)
+        for start in range(cols.start, cols.stop, LANES):
+            lanes = slice(start, start + LANES)
+            for at in range(part.start, part.stop, per_req):
+                here = slice(at, at + per_req)
+                pair = at % devices // per_req // 2 * 8
+                places = [request[n : n + 8, :][:, :, None] for n in (at, at + 8)]
+                factor = mixed[
+                    at - part.start : at - part.start + per_req,
+                    start - cols.start : start - cols.start + LANES,
+                ]
+                factor = factor + of_request(shift[pair : pair + 8, lanes], places)
+                if start < user_width:
+                    own = of_request(users[start // LANES, pair : pair + 8, :], places)
+                    first[here, lanes] = own.astype(BF)
+                else:
+                    own = first[here, lanes].astype(F32)
+                new = own * factor
+                state[here, lanes] = new
+                state_one[here, lanes] = new.astype(BF)
+
+    request_term(0)
+    for n, cols in enumerate(columns):
+        layer_one(parts[0], cols)
+        if n + 1 < count:
+            request_term(n + 1)
+        else:
+            cross_two_here.wait()
+            hidden_here.start()
+        if n == 0:
+            cross_two_here.start()
+        layer_one(parts[1], cols)
     for part in parts:
+        if part.start > 0:
+            hidden_here.wait()
         for cols in tiles(cross):
-            factor = jnp.dot(
-                first[part, user_width:],
-                cross_item[:, cols],
-                preferred_element_type=F32,
-            )
-            factor += jnp.dot(users_hot[part, :], shift[:, cols], preferred_element_type=F32)
-            new = first[part, cols].astype(F32) * factor
-            state[part, cols] = new
-            state_one[part, cols] = new.astype(BF)
-    cross_two_here.wait()
-    for part in parts:
-        for cols in tiles(cross):
-            mixed = jnp.dot(
-                state_one[part, :], cross_two[:, cols], preferred_element_type=F32
-            )
+            mixed = jnp.dot(state_one[part, :], cross_two[:, cols], preferred_element_type=F32)
             mixed += cross_bias_ref[1:2, cols]
             new = first[part, cols].astype(F32) * mixed + state[part, cols]
             state_two[part, cols] = new.astype(BF)
-    hidden_here.wait()
     lane = iota((devices, LANES), 1)
     total = jnp.zeros((devices, LANES), F32)
     for part in range(2):
@@ -276,12 +323,12 @@
             pltpu.VMEM((item_width, cross), BF),
             pltpu.VMEM((cross, cross), BF),
             pltpu.VMEM((cross, hid), BF),
-            pltpu.SemaphoreType.DMA((5,)),
+            pltpu.SemaphoreType.DMA((11,)),
             pltpu.VMEM((devices * WORDS, LANES), F32),
-            pltpu.VMEM((32, user_width), F32),
-            pltpu.VMEM((LANES, cross), BF),
+            pltpu.VMEM((user_width // LANES, 32, LANES), F32),
+            pltpu.VMEM((32, cross), F32),
+            pltpu.VMEM((slots, LANES), jnp.int32),
             pltpu.VMEM((slots, table_slab.shape[0]), BF),
-            pltpu.VMEM((slots, LANES), BF),
             pltpu.VMEM((slots, cross), BF),
             pltpu.VMEM((slots, cross), F32),
             pltpu.VMEM((slots, cross), BF),

time: 62.7 us -> 61.9 us (0.987)
  Pallas kernels: 27.2 us -> 26.4 us
    pallas_call x1, Pallas kernels: 24.3 us -> 23.5 us  [per_device(): pl.pallas_call(score_kernel, out_shape=pltpu.VMEM((devices, LANES), F32),...]
where the time goes in v5:
time: 61.9 us; the launch traced here: 61.7 us
  blocking collectives  35.3 us (57%)
  Pallas kernels  26.4 us (43%)
    pallas_call x1, Pallas kernels, per_device(): pl.pallas_call(score_kernel, out_shape=pltpu.VMEM((devices, LANES), F32),...  23.5 us
    all_to_all x1, blocking collectives, per_device(): asked = lax.all_to_all(msg, AXES, split_axis=0, concat_axis=0, tiled=True)  21.7 us
    all_to_all x1, blocking collectives, per_device(): lax.all_to_all(scores, AXES, split_axis=0, concat_axis=0, tiled=True)  13.6 us
    pallas_call x1, Pallas kernels, per_device(): pl.pallas_call(prepare_kernel, out_shape=(jax.ShapeDtypeStruct((devices *...  1.93 us

profile of v5, /device:TPU:1, one launch (start us, length us, event | category | flops | bytes accessed | tf_op | source)
XLA Modules:
  0.0 61.7 jit_solution(17500365385206193234)
XLA Ops:
  0.0 1.9 %prepare.1 = (bf16[512,128]{1,0:T(8,128)(2,1)S(1)}, s32[4,128]{1,0:T(4,128)S(1)}, bf16[1024,512]{1,0:T(8,128)(2,1)S(1)}) custom-call(s32[4,128]{1,0:T(4,128)} %ids_ref.1, bf16[4,64]{1,0:T(4,128)(2,1)} %user_ref.1, bf16[1024,1024]{1,0:T(8,128)(2,1)} %slab_hbm.3), custom_call_target="tpu_custom_call" | custom-call | tf_op jit(solution)/shard_map/prepare/pallas_call | solution.py:298
  1.9 21.7 %all_to_all.22 = bf16[128,4,128]{2,1,0:T(4,128)(2,1)S(1)} all-to-all(bf16[128,4,128]{2,1,0:T(4,128)(2,1)S(1)} %bitcast.11), channel_id=1, replica_groups=mesh['req'=8,'score'=16] {'req','score'}, dimensions={0} | all-to-all | bytes 262144 | tf_op jit(solution)/shard_map/all_to_all | solution.py:314
  23.6 23.5 %score.1 = f32[128,128]{1,0:T(8,128)S(1)} custom-call(bf16[512,128]{1,0:T(8,128)(2,1)S(1)} %bitcast.8, bf16[1024,512]{1,0:T(8,128)(2,1)S(1)} %get-tuple-element.9.slab_ref, bf16[1024,1024]{1,0:T(8,128)(2,1)} %slab_hbm.3, bf16[2,2048,2048]{2,1,0:T(8,128)(2,1)} %cross_hbm.1, f32[2,2048]{1,0:T(2,128)} %cross_bias_ref.1, bf16[2048,1024]{1,0:T(8,128)(2,1)} %hidden_hbm.1, ...), custom_call_target="tpu_custom_call" | custom-call | tf_op jit(solution)/shard_map/score/pallas_call | solution.py:315
  47.2 13.6 %all_to_all.23 = f32[128,1,128]{2,1,0:T(1,128)S(1)} all-to-all(f32[128,1,128]{2,1,0:T(1,128)S(1)} %bitcast.9), channel_id=1, replica_groups=mesh['req'=8,'score'=16] {'req','score'}, dimensions={0} | all-to-all | bytes 131072 | tf_op jit(solution)/shard_map/all_to_all | solution.py:349
  60.7 1.0 %collect.1 = f32[4,128]{1,0:T(4,128)} custom-call(f32[128,128]{1,0:T(8,128)S(1)} %bitcast.10, s32[4,128]{1,0:T(4,128)S(1)} %get-tuple-element.10.key_ref), custom_call_target="tpu_custom_call" | custom-call | tf_op jit(solution)/shard_map/collect/pallas_call | solution.py:350

commit v6 on v5

--- a/solution.py
+++ b/solution.py
@@ -22,12 +22,26 @@
 
 
 def prepare_kernel(
-    ids_ref, user_ref, slab_hbm, msg_ref, key_ref, slab_ref, wide, copied
+    ids_hbm,
+    user_hbm,
+    slab_hbm,
+    msg_ref,
+    key_ref,
+    slab_ref,
+    ids_ref,
+    user_ref,
+    wide,
+    copied,
 ):
+    ids_here = pltpu.make_async_copy(ids_hbm, ids_ref, copied.at[0])
+    user_here = pltpu.make_async_copy(user_hbm, user_ref, copied.at[1])
     slab_here = pltpu.make_async_copy(
-        slab_hbm.at[:, pl.ds(0, slab_ref.shape[1])], slab_ref, copied
-    )
+        slab_hbm.at[:, pl.ds(0, slab_ref.shape[1])], slab_ref, copied.at[2]
+    )
+    ids_here.start()
+    user_here.start()
     slab_here.start()
+    ids_here.wait()
     groups, width = ids_ref.shape
     devices = msg_ref.shape[0] // WORDS
     ids = ids_ref[...]
@@ -36,8 +50,7 @@
     upto = (iota((width, width), 0) <= iota((width, width), 1)).astype(BF)
     device_row = iota((devices, width), 0)
     base = jnp.zeros((devices, 1), F32)
-    high = jnp.zeros((devices, LANES), F32)
-    low = jnp.zeros((devices, LANES), F32)
+    slot_values = jnp.zeros((devices, LANES), F32)
     contract_last = (((1,), (1,)), ((), ()))
     for q in range(groups):
         mine = device_row == owner[q : q + 1, :]
@@ -47,21 +60,23 @@
         rank = rank.astype(jnp.int32)
         base = count[:, width - 1 : width]
         value = local[q : q + 1, :] * groups + (q + 1)
-        at_rank = iota((LANES, width), 0) == rank
-        value_high = jnp.where(at_rank, value >> 4, 0).astype(F32).astype(BF)
-        value_low = jnp.where(at_rank, value & 15, 0).astype(F32).astype(BF)
-        high += lax.dot_general(onehot, value_high, contract_last, preferred_element_type=F32)
-        low += lax.dot_general(onehot, value_low, contract_last, preferred_element_type=F32)
+        place = iota((LANES, width), 0)
+        digit = jnp.where(place == rank, value >> 4, 0)
+        digit = jnp.where(place == rank + CAP, value & 15, digit)
+        slot_values += lax.dot_general(
+            onehot, digit.astype(F32).astype(BF), contract_last, preferred_element_type=F32
+        )
         key_ref[q : q + 1, :] = owner[q : q + 1, :] * CAP + rank
+    user_here.wait()
     user = user_ref[...].astype(F32)
     pairs = [
         jnp.concatenate([user[2 * p : 2 * p + 1, :], user[2 * p + 1 : 2 * p + 2, :]], axis=1)
         for p in range(2)
     ]
-    wide[pl.ds(0, devices, stride=WORDS), :] = high
+    wide[pl.ds(0, devices, stride=WORDS), :] = slot_values
     for p in range(2):
         wide[pl.ds(p + 1, devices, stride=WORDS), :] = jnp.broadcast_to(pairs[p], (devices, LANES))
-    wide[pl.ds(3, devices, stride=WORDS), :] = low
+    wide[pl.ds(3, devices, stride=WORDS), :] = jnp.zeros((devices, LANES), F32)
     msg_ref[...] = wide[...].astype(BF)
     slab_here.wait()
 
@@ -106,8 +121,8 @@
     tile = 512
     parts = [slice(h, h + half) for h in range(0, slots, half)]
 
-    def tiles(width):
-        return [slice(n, n + tile) for n in range(0, width, tile)]
+    def tiles(width, size=tile):
+        return [slice(n, n + size) for n in range(0, width, size)]
 
     def copy(i, source, target):
         return pltpu.make_async_copy(source, target, copied.at[i])
@@ -142,8 +157,17 @@
                 items_hot[part, :], table[:, cols], preferred_element_type=F32
             ).astype(BF)
 
-    value = wide[pl.ds(0, devices, stride=WORDS), :] * 16.0
-    value += wide[pl.ds(3, devices, stride=WORDS), :]
+    left = iota((8, LANES), 1) < 64
+    for t in range(user_width // LANES):
+        for p in range(2):
+            even = wide[pl.ds(8 * t + 1 + p, 8, stride=WORDS * per_req), :]
+            odd = wide[pl.ds(8 * t + 5 + p, 8, stride=WORDS * per_req), :]
+            users[t, pl.ds(2 * p, 8, stride=4), :] = jnp.where(left, even, pltpu.roll(odd, 64, 1))
+            users[t, pl.ds(2 * p + 1, 8, stride=4), :] = jnp.where(
+                left, pltpu.roll(even, 64, 1), odd
+            )
+    value = wide[pl.ds(0, devices, stride=WORDS), :]
+    value = value * 16.0 + pltpu.roll(value, LANES - CAP, 1)
     value = value.astype(jnp.int32) - 1
     row_of = value >> 2
     req_of = (value & 3) + (iota((devices, LANES), 0) // per_req & 1) * 4
@@ -154,15 +178,6 @@
             items_hot[here, :] = (row_lane == row_of[:, k : k + 1]).astype(BF)
             request[here, :] = jnp.broadcast_to(req_of[:, k : k + 1], (devices, LANES))
         fetch(part, slab_ref, user_width)
-    left = iota((8, LANES), 1) < 64
-    for t in range(user_width // LANES):
-        for p in range(2):
-            even = wide[pl.ds(8 * t + 1 + p, 8, stride=WORDS * per_req), :]
-            odd = wide[pl.ds(8 * t + 5 + p, 8, stride=WORDS * per_req), :]
-            users[t, pl.ds(2 * p, 8, stride=4), :] = jnp.where(left, even, pltpu.roll(odd, 64, 1))
-            users[t, pl.ds(2 * p + 1, 8, stride=4), :] = jnp.where(
-                left, pltpu.roll(even, 64, 1), odd
-            )
     slab_here.wait()
     for part in parts:
         fetch(part, slab_rest, user_width + staged)
@@ -190,12 +205,14 @@
         ]
         return jnp.concatenate(got, axis=0)
 
-    def request_term(n):
-        user_here[n].wait()
-        item_here[n].wait()
-        cols = columns[n]
-        base = jnp.dot(users_bf, cross_user[:, cols], preferred_element_type=F32)
-        shift[:, cols] = base + (cross_bias_ref[0:1, cols] + 1.0)
+    def request_term(places):
+        for n in places:
+            user_here[n].wait()
+            item_here[n].wait()
+        for n in places:
+            cols = columns[n]
+            base = jnp.dot(users_bf, cross_user[:, cols], preferred_element_type=F32)
+            shift[:, cols] = base + (cross_bias_ref[0:1, cols] + 1.0)
 
     def layer_one(part, cols):
         mixed = jnp.dot(first[part, user_width:], cross_item[:, cols], preferred_element_type=F32)
@@ -219,21 +236,20 @@
                 state[here, lanes] = new
                 state_one[here, lanes] = new.astype(BF)
 
-    request_term(0)
+    request_term([0])
     for n, cols in enumerate(columns):
         layer_one(parts[0], cols)
-        if n + 1 < count:
-            request_term(n + 1)
-        else:
-            cross_two_here.wait()
-            hidden_here.start()
         if n == 0:
             cross_two_here.start()
+            hidden_here.start()
+            request_term(range(1, count))
+        if n == count - 1:
+            cross_two_here.wait()
         layer_one(parts[1], cols)
     for part in parts:
         if part.start > 0:
             hidden_here.wait()
-        for cols in tiles(cross):
+        for cols in tiles(cross, 2 * tile):
             mixed = jnp.dot(state_one[part, :], cross_two[:, cols], preferred_element_type=F32)
             mixed += cross_bias_ref[1:2, cols]
             new = first[part, cols].astype(F32) * mixed + state[part, cols]
@@ -242,18 +258,23 @@
     total = jnp.zeros((devices, LANES), F32)
     for part in range(2):
         gathered = jnp.zeros((half, LANES), F32)
-        for start in range(0, hid, tile):
-            cols = slice(start, start + tile)
+        sizes = [tile] * (hid // tile)
+        if part == 1:
+            sizes = sizes[:-1] + [tile // 2] * 2
+        start = 0
+        for size in sizes:
+            cols = slice(start, start + size)
             hidden = jnp.dot(
                 state_two[part * half : (part + 1) * half, :],
                 hidden_ref[:, cols],
                 preferred_element_type=F32,
             )
-            for j in range(tile // LANES):
+            for j in range(size // LANES):
                 at = start // LANES + j
                 unit = hidden[:, j * LANES : (j + 1) * LANES] + hidden_bias_ref[at : at + 1, :]
                 unit = jnp.maximum(unit, 0.0).astype(BF).astype(F32)
                 gathered += unit * out_ref[at : at + 1, :].astype(F32)
+            start += size
         logit = jnp.sum(gathered, axis=1, keepdims=True)
         for k in range(half_ranks):
             here = lane == part * half_ranks + k
@@ -265,13 +286,16 @@
     groups, width = key_ref.shape
     devices = scores_ref.shape[0]
     scores = scores_ref[...]
+    of_rank = [jnp.broadcast_to(scores[:, k : k + 1], (devices, width)) for k in range(CAP)]
+    device = iota((devices, width), 0)
     for q in range(groups):
         key = key_ref[q : q + 1, :]
-        total = jnp.zeros((devices, width), F32)
-        for k in range(CAP):
-            here = iota((devices, width), 0) * CAP + k == key
-            total += jnp.where(here, scores[:, k : k + 1], 0.0)
-        out_ref[q : q + 1, :] = jnp.sum(total, axis=0, keepdims=True)
+        rank = key & (CAP - 1)
+        got = of_rank[0]
+        for k in range(1, CAP):
+            got = jnp.where(rank == k, of_rank[k], got)
+        got = jnp.where(device == key >> 3, got, 0.0)
+        out_ref[q : q + 1, :] = jnp.sum(got, axis=0, keepdims=True)
 
 
 def per_device(
@@ -302,11 +326,13 @@
             jax.ShapeDtypeStruct((groups, width), jnp.int32),
             pltpu.VMEM((table_slab.shape[0], staged), BF),
         ),
-        in_specs=[vmem, vmem, hbm],
+        in_specs=[hbm, hbm, hbm],
         out_specs=(vmem, vmem, vmem),
         scratch_shapes=[
+            pltpu.VMEM(cand_ids.shape, jnp.int32),
+            pltpu.VMEM(user_rows.shape, BF),
             pltpu.VMEM((devices * WORDS, LANES), F32),
-            pltpu.SemaphoreType.DMA,
+            pltpu.SemaphoreType.DMA((3,)),
         ],
         compiler_params=pltpu.CompilerParams(vmem_limit_bytes=16 * 2**20),
         name="prepare",

time: 61.9 us -> 61.5 us (level)
  no operation moved by 1% of the time
where the time goes in v6:
time: 61.5 us; the launch traced here: 61.3 us
  blocking collectives  35.3 us (57%)
  Pallas kernels  26 us (42%)
    pallas_call x1, Pallas kernels, per_device(): pl.pallas_call(score_kernel, out_shape=pltpu.VMEM((devices, LANES), F32),...  23.7 us
    all_to_all x1, blocking collectives, per_device(): asked = lax.all_to_all(msg, AXES, split_axis=0, concat_axis=0, tiled=True)  21.7 us
    all_to_all x1, blocking collectives, per_device(): lax.all_to_all(scores, AXES, split_axis=0, concat_axis=0, tiled=True)  13.6 us
    pallas_call x1, Pallas kernels, per_device(): pl.pallas_call(prepare_kernel, out_shape=(jax.ShapeDtypeStruct((devices *...  1.48 us

profile of v6, /device:TPU:1, one launch (start us, length us, event | category | flops | bytes accessed | tf_op | source)
XLA Modules:
  0.0 61.3 jit_solution(17345379220482933407)
XLA Ops:
  0.0 1.5 %prepare.1 = (bf16[512,128]{1,0:T(8,128)(2,1)S(1)}, s32[4,128]{1,0:T(4,128)S(1)}, bf16[1024,512]{1,0:T(8,128)(2,1)S(1)}) custom-call(s32[4,128]{1,0:T(4,128)} %ids_hbm.1, bf16[4,64]{1,0:T(4,128)(2,1)} %user_hbm.1, bf16[1024,1024]{1,0:T(8,128)(2,1)} %slab_hbm.3), custom_call_target="tpu_custom_call" | custom-call | tf_op jit(solution)/shard_map/prepare/pallas_call | solution.py:322
  1.5 21.7 %all_to_all.22 = bf16[128,4,128]{2,1,0:T(4,128)(2,1)S(1)} all-to-all(bf16[128,4,128]{2,1,0:T(4,128)(2,1)S(1)} %bitcast.11), channel_id=1, replica_groups=mesh['req'=8,'score'=16] {'req','score'}, dimensions={0} | all-to-all | bytes 262144 | tf_op jit(solution)/shard_map/all_to_all | solution.py:340
  23.2 23.7 %score.1 = f32[128,128]{1,0:T(8,128)S(1)} custom-call(bf16[512,128]{1,0:T(8,128)(2,1)S(1)} %bitcast.8, bf16[1024,512]{1,0:T(8,128)(2,1)S(1)} %get-tuple-element.9.slab_ref, bf16[1024,1024]{1,0:T(8,128)(2,1)} %slab_hbm.3, bf16[2,2048,2048]{2,1,0:T(8,128)(2,1)} %cross_hbm.1, f32[2,2048]{1,0:T(2,128)} %cross_bias_ref.1, bf16[2048,1024]{1,0:T(8,128)(2,1)} %hidden_hbm.1, ...), custom_call_target="tpu_custom_call" | custom-call | tf_op jit(solution)/shard_map/score/pallas_call | solution.py:341
  46.9 13.6 %all_to_all.23 = f32[128,1,128]{2,1,0:T(1,128)S(1)} all-to-all(f32[128,1,128]{2,1,0:T(1,128)S(1)} %bitcast.9), channel_id=1, replica_groups=mesh['req'=8,'score'=16] {'req','score'}, dimensions={0} | all-to-all | bytes 131072 | tf_op jit(solution)/shard_map/all_to_all | solution.py:375
  60.5 0.8 %collect.1 = f32[4,128]{1,0:T(4,128)} custom-call(f32[128,128]{1,0:T(8,128)S(1)} %bitcast.10, s32[4,128]{1,0:T(4,128)S(1)} %get-tuple-element.10.key_ref), custom_call_target="tpu_custom_call" | custom-call | tf_op jit(solution)/shard_map/collect/pallas_call | solution.py:376

commit v7 on v6

--- a/solution.py
+++ b/solution.py
@@ -121,8 +121,8 @@
     tile = 512
     parts = [slice(h, h + half) for h in range(0, slots, half)]
 
-    def tiles(width, size=tile):
-        return [slice(n, n + size) for n in range(0, width, size)]
+    def tiles(width):
+        return [slice(n, n + tile) for n in range(0, width, tile)]
 
     def copy(i, source, target):
         return pltpu.make_async_copy(source, target, copied.at[i])
@@ -157,15 +157,6 @@
                 items_hot[part, :], table[:, cols], preferred_element_type=F32
             ).astype(BF)
 
-    left = iota((8, LANES), 1) < 64
-    for t in range(user_width // LANES):
-        for p in range(2):
-            even = wide[pl.ds(8 * t + 1 + p, 8, stride=WORDS * per_req), :]
-            odd = wide[pl.ds(8 * t + 5 + p, 8, stride=WORDS * per_req), :]
-            users[t, pl.ds(2 * p, 8, stride=4), :] = jnp.where(left, even, pltpu.roll(odd, 64, 1))
-            users[t, pl.ds(2 * p + 1, 8, stride=4), :] = jnp.where(
-                left, pltpu.roll(even, 64, 1), odd
-            )
     value = wide[pl.ds(0, devices, stride=WORDS), :]
     value = value * 16.0 + pltpu.roll(value, LANES - CAP, 1)
     value = value.astype(jnp.int32) - 1
@@ -178,6 +169,15 @@
             items_hot[here, :] = (row_lane == row_of[:, k : k + 1]).astype(BF)
             request[here, :] = jnp.broadcast_to(req_of[:, k : k + 1], (devices, LANES))
         fetch(part, slab_ref, user_width)
+    left = iota((8, LANES), 1) < 64
+    for t in range(user_width // LANES):
+        for p in range(2):
+            even = wide[pl.ds(8 * t + 1 + p, 8, stride=WORDS * per_req), :]
+            odd = wide[pl.ds(8 * t + 5 + p, 8, stride=WORDS * per_req), :]
+            users[t, pl.ds(2 * p, 8, stride=4), :] = jnp.where(left, even, pltpu.roll(odd, 64, 1))
+            users[t, pl.ds(2 * p + 1, 8, stride=4), :] = jnp.where(
+                left, pltpu.roll(even, 64, 1), odd
+            )
     slab_here.wait()
     for part in parts:
         fetch(part, slab_rest, user_width + staged)
@@ -249,7 +249,7 @@
     for part in parts:
         if part.start > 0:
             hidden_here.wait()
-        for cols in tiles(cross, 2 * tile):
+        for cols in tiles(cross):
             mixed = jnp.dot(state_one[part, :], cross_two[:, cols], preferred_element_type=F32)
             mixed += cross_bias_ref[1:2, cols]
             new = first[part, cols].astype(F32) * mixed + state[part, cols]
@@ -258,23 +258,18 @@
     total = jnp.zeros((devices, LANES), F32)
     for part in range(2):
         gathered = jnp.zeros((half, LANES), F32)
-        sizes = [tile] * (hid // tile)
-        if part == 1:
-            sizes = sizes[:-1] + [tile // 2] * 2
-        start = 0
-        for size in sizes:
-            cols = slice(start, start + size)
+        for start in range(0, hid, tile):
+            cols = slice(start, start + tile)
             hidden = jnp.dot(
                 state_two[part * half : (part + 1) * half, :],
                 hidden_ref[:, cols],
                 preferred_element_type=F32,
             )
-            for j in range(size // LANES):
+            for j in range(tile // LANES):
                 at = start // LANES + j
                 unit = hidden[:, j * LANES : (j + 1) * LANES] + hidden_bias_ref[at : at + 1, :]
                 unit = jnp.maximum(unit, 0.0).astype(BF).astype(F32)
                 gathered += unit * out_ref[at : at + 1, :].astype(F32)
-            start += size
         logit = jnp.sum(gathered, axis=1, keepdims=True)
         for k in range(half_ranks):
             here = lane == part * half_ranks + k

time: 61.5 us -> 61.3 us (level)
  no operation moved by 1% of the time
where the time goes in v7:
time: 61.3 us; the launch traced here: 61.1 us
  blocking collectives  35.3 us (58%)
  Pallas kernels  25.8 us (42%)
    pallas_call x1, Pallas kernels, per_device(): pl.pallas_call(score_kernel, out_shape=pltpu.VMEM((devices, LANES), F32),...  23.5 us
    all_to_all x1, blocking collectives, per_device(): asked = lax.all_to_all(msg, AXES, split_axis=0, concat_axis=0, tiled=True)  21.7 us
    all_to_all x1, blocking collectives, per_device(): lax.all_to_all(scores, AXES, split_axis=0, concat_axis=0, tiled=True)  13.6 us
    pallas_call x1, Pallas kernels, per_device(): pl.pallas_call(prepare_kernel, out_shape=(jax.ShapeDtypeStruct((devices *...  1.48 us

profile of v7, /device:TPU:1, one launch (start us, length us, event | category | flops | bytes accessed | tf_op | source)
XLA Modules:
  0.0 61.1 jit_solution(5443529358669004428)
XLA Ops:
  0.0 1.5 %prepare.1 = (bf16[512,128]{1,0:T(8,128)(2,1)S(1)}, s32[4,128]{1,0:T(4,128)S(1)}, bf16[1024,512]{1,0:T(8,128)(2,1)S(1)}) custom-call(s32[4,128]{1,0:T(4,128)} %ids_hbm.1, bf16[4,64]{1,0:T(4,128)(2,1)} %user_hbm.1, bf16[1024,1024]{1,0:T(8,128)(2,1)} %slab_hbm.3), custom_call_target="tpu_custom_call" | custom-call | tf_op jit(solution)/shard_map/prepare/pallas_call | solution.py:317
  1.5 21.7 %all_to_all.22 = bf16[128,4,128]{2,1,0:T(4,128)(2,1)S(1)} all-to-all(bf16[128,4,128]{2,1,0:T(4,128)(2,1)S(1)} %bitcast.11), channel_id=1, replica_groups=mesh['req'=8,'score'=16] {'req','score'}, dimensions={0} | all-to-all | bytes 262144 | tf_op jit(solution)/shard_map/all_to_all | solution.py:335
  23.2 23.5 %score.1 = f32[128,128]{1,0:T(8,128)S(1)} custom-call(bf16[512,128]{1,0:T(8,128)(2,1)S(1)} %bitcast.8, bf16[1024,512]{1,0:T(8,128)(2,1)S(1)} %get-tuple-element.9.slab_ref, bf16[1024,1024]{1,0:T(8,128)(2,1)} %slab_hbm.3, bf16[2,2048,2048]{2,1,0:T(8,128)(2,1)} %cross_hbm.1, f32[2,2048]{1,0:T(2,128)} %cross_bias_ref.1, bf16[2048,1024]{1,0:T(8,128)(2,1)} %hidden_hbm.1, ...), custom_call_target="tpu_custom_call" | custom-call | tf_op jit(solution)/shard_map/score/pallas_call | solution.py:336
  46.7 13.6 %all_to_all.23 = f32[128,1,128]{2,1,0:T(1,128)S(1)} all-to-all(f32[128,1,128]{2,1,0:T(1,128)S(1)} %bitcast.9), channel_id=1, replica_groups=mesh['req'=8,'score'=16] {'req','score'}, dimensions={0} | all-to-all | bytes 131072 | tf_op jit(solution)/shard_map/all_to_all | solution.py:370
  60.2 0.8 %collect.1 = f32[4,128]{1,0:T(4,128)} custom-call(f32[128,128]{1,0:T(8,128)S(1)} %bitcast.10, s32[4,128]{1,0:T(4,128)S(1)} %get-tuple-element.10.key_ref), custom_call_target="tpu_custom_call" | custom-call | tf_op jit(solution)/shard_map/collect/pallas_call | solution.py:371

commit v8 on v7

--- a/solution.py
+++ b/solution.py
@@ -77,7 +77,7 @@
     for p in range(2):
         wide[pl.ds(p + 1, devices, stride=WORDS), :] = jnp.broadcast_to(pairs[p], (devices, LANES))
     wide[pl.ds(3, devices, stride=WORDS), :] = jnp.zeros((devices, LANES), F32)
-    msg_ref[...] = wide[...].astype(BF)
+    msg_ref[...] = wide[: msg_ref.shape[0], :].astype(BF)
     slab_here.wait()
 
 
@@ -149,7 +149,7 @@
     for n in range(count):
         user_here[n].start()
         item_here[n].start()
-    wide[...] = msg_ref[...].astype(F32)
+    wide[: msg_ref.shape[0], :] = msg_ref[...].astype(F32)
 
     def fetch(part, table, at):
         for cols in tiles(table.shape[1]):
@@ -182,7 +182,7 @@
     for part in parts:
         fetch(part, slab_rest, user_width + staged)
     users_bf = jnp.concatenate(
-        [users[t].astype(BF) for t in range(user_width // LANES)], axis=1
+        [users[t, :32, :].astype(BF) for t in range(user_width // LANES)], axis=1
     )
     along_rows = lax.GatherDimensionNumbers(
         offset_dims=(),
@@ -326,7 +326,7 @@
         scratch_shapes=[
             pltpu.VMEM(cand_ids.shape, jnp.int32),
             pltpu.VMEM(user_rows.shape, BF),
-            pltpu.VMEM((devices * WORDS, LANES), F32),
+            pltpu.VMEM((devices * WORDS + 16 * WORDS, LANES), F32),
             pltpu.SemaphoreType.DMA((3,)),
         ],
         compiler_params=pltpu.CompilerParams(vmem_limit_bytes=16 * 2**20),
@@ -345,8 +345,8 @@
             pltpu.VMEM((cross, cross), BF),
             pltpu.VMEM((cross, hid), BF),
             pltpu.SemaphoreType.DMA((11,)),
-            pltpu.VMEM((devices * WORDS, LANES), F32),
-            pltpu.VMEM((user_width // LANES, 32, LANES), F32),
+            pltpu.VMEM((devices * WORDS + 16 * WORDS, LANES), F32),
+            pltpu.VMEM((user_width // LANES, 40, LANES), F32),
             pltpu.VMEM((32, cross), F32),
             pltpu.VMEM((slots, LANES), jnp.int32),
             pltpu.VMEM((slots, table_slab.shape[0]), BF),

time: 61.3 us -> 61.3 us (level)
  no operation moved by 1% of the time
where the time goes in v8:
time: 61.3 us; the launch traced here: 61.1 us
  blocking collectives  35.3 us (58%)
  Pallas kernels  25.8 us (42%)
    pallas_call x1, Pallas kernels, per_device(): pl.pallas_call(score_kernel, out_shape=pltpu.VMEM((devices, LANES), F32),...  23.5 us
    all_to_all x1, blocking collectives, per_device(): asked = lax.all_to_all(msg, AXES, split_axis=0, concat_axis=0, tiled=True)  21.7 us
    all_to_all x1, blocking collectives, per_device(): lax.all_to_all(scores, AXES, split_axis=0, concat_axis=0, tiled=True)  13.6 us
    pallas_call x1, Pallas kernels, per_device(): pl.pallas_call(prepare_kernel, out_shape=(jax.ShapeDtypeStruct((devices *...  1.48 us

profile of v8, /device:TPU:1, one launch (start us, length us, event | category | flops | bytes accessed | tf_op | source)
XLA Modules:
  0.0 61.1 jit_solution(11197319758431045715)
XLA Ops:
  0.0 1.5 %prepare.1 = (bf16[512,128]{1,0:T(8,128)(2,1)S(1)}, s32[4,128]{1,0:T(4,128)S(1)}, bf16[1024,512]{1,0:T(8,128)(2,1)S(1)}) custom-call(s32[4,128]{1,0:T(4,128)} %ids_hbm.1, bf16[4,64]{1,0:T(4,128)(2,1)} %user_hbm.1, bf16[1024,1024]{1,0:T(8,128)(2,1)} %slab_hbm.3), custom_call_target="tpu_custom_call" | custom-call | tf_op jit(solution)/shard_map/prepare/pallas_call | solution.py:317
  1.5 21.7 %all_to_all.22 = bf16[128,4,128]{2,1,0:T(4,128)(2,1)S(1)} all-to-all(bf16[128,4,128]{2,1,0:T(4,128)(2,1)S(1)} %bitcast.11), channel_id=1, replica_groups=mesh['req'=8,'score'=16] {'req','score'}, dimensions={0} | all-to-all | bytes 262144 | tf_op jit(solution)/shard_map/all_to_all | solution.py:335
  23.2 23.5 %score.1 = f32[128,128]{1,0:T(8,128)S(1)} custom-call(bf16[512,128]{1,0:T(8,128)(2,1)S(1)} %bitcast.8, bf16[1024,512]{1,0:T(8,128)(2,1)S(1)} %get-tuple-element.9.slab_ref, bf16[1024,1024]{1,0:T(8,128)(2,1)} %slab_hbm.3, bf16[2,2048,2048]{2,1,0:T(8,128)(2,1)} %cross_hbm.1, f32[2,2048]{1,0:T(2,128)} %cross_bias_ref.1, bf16[2048,1024]{1,0:T(8,128)(2,1)} %hidden_hbm.1, ...), custom_call_target="tpu_custom_call" | custom-call | tf_op jit(solution)/shard_map/score/pallas_call | solution.py:336
  46.7 13.6 %all_to_all.23 = f32[128,1,128]{2,1,0:T(1,128)S(1)} all-to-all(f32[128,1,128]{2,1,0:T(1,128)S(1)} %bitcast.9), channel_id=1, replica_groups=mesh['req'=8,'score'=16] {'req','score'}, dimensions={0} | all-to-all | bytes 131072 | tf_op jit(solution)/shard_map/all_to_all | solution.py:370
  60.2 0.8 %collect.1 = f32[4,128]{1,0:T(4,128)} custom-call(f32[128,128]{1,0:T(8,128)S(1)} %bitcast.10, s32[4,128]{1,0:T(4,128)S(1)} %get-tuple-element.10.key_ref), custom_call_target="tpu_custom_call" | custom-call | tf_op jit(solution)/shard_map/collect/pallas_call | solution.py:371
